TPU v7x, 32 devices: a whole 2x2x4 slice. The times are simulated.
32 devices in a mesh: dp: 4 (over x, core), expert: 8 (over z, y).
Axes of the slice: x: 2, y: 2, z: 4, core: 2. Of those that a mesh axis runs over, the one named last changes fastest.
Arguments:
- tokens: bfloat16 [2048, 7168], P('expert', 'dp'), may hold values from -6 to 6
- grad_out: bfloat16 [2048, 7168], P('expert', 'dp'), may hold values from -6 to 6
- route_ids: int32 [2048, 8], P('expert'), may hold values from 0 to 255, all different within a row; in each aligned block of 256 rows (0 to 255, 256 to 511, ...) at most 12 rows name the same one
- route_gates: float32 [2048, 8], P('expert'), may hold values from 0.1 to 1
- w_gate: bfloat16 [8, 7168, 1024], P('expert', 'dp'), may hold values from -0.0625 to 0.0625
- w_up: bfloat16 [8, 7168, 1024], P('expert', 'dp'), may hold values from -0.0625 to 0.0625
- w_down: bfloat16 [8, 1024, 7168], P('expert', None, 'dp'), may hold values from -0.1875 to 0.1875
- shared_gate: bfloat16 [7168, 1024], P('dp', 'expert'), may hold values from -0.0625 to 0.0625
- shared_up: bfloat16 [7168, 1024], P('dp', 'expert'), may hold values from -0.0625 to 0.0625
- shared_down: bfloat16 [1024, 7168], P('expert', 'dp'), may hold values from -0.1875 to 0.1875
Outputs:
- grad_tokens: bfloat16 [2048, 7168], P('expert', 'dp')
- grad_gate: bfloat16 [8, 7168, 1024], P('expert', 'dp')
- grad_up: bfloat16 [8, 7168, 1024], P('expert', 'dp')
- grad_down: bfloat16 [8, 1024, 7168], P('expert', None, 'dp')
- grad_shared_gate: float32 [7168, 1024], P('dp', 'expert')
- grad_shared_up: float32 [7168, 1024], P('dp', 'expert')
- grad_shared_down: float32 [1024, 7168], P('expert', 'dp')
Inputs may be any that keep to these rules, and one draw needn't show every extreme that they name: `route_ids`: each row names 8 different experts; in each aligned block of 256 rows no expert is named by more than 12 rows, a bound that some block reaches.
All inputs are finite; a program needn't handle non-finite values.
Results may differ from a plain program's by a relative error of at most 0.018.
Values may be sent and summed in bfloat16 or wider, within the bound.
A program may use at most 128 MiB of HBM per device.

v0:
```python
import jax
import jax.numpy as jnp
from jax import lax
from jax.sharding import PartitionSpec as P

CAP = 12


def silu_parts(pre):
    sigmoid_val = jax.nn.sigmoid(pre)
    return (pre * sigmoid_val, sigmoid_val * (1.0 + pre * (1.0 - sigmoid_val)))


def contract_rows(left, right):
    return lax.dot_general(
        left, right, (((0,), (0,)), ((), ())), preferred_element_type=jnp.float32
    )


def contract_cols(left, right):
    return lax.dot_general(
        left, right, (((1,), (1,)), ((), ())), preferred_element_type=jnp.float32
    )


def hidden_products(part_gate, part_up, part_act):
    silu_val, silu_slope = silu_parts(part_gate)
    activated = (silu_val * part_up).astype(jnp.bfloat16)
    grad_gate_pre = (part_act * part_up * silu_slope).astype(jnp.bfloat16)
    grad_up_pre = (part_act * silu_val).astype(jnp.bfloat16)
    return (activated, grad_gate_pre, grad_up_pre)


def expert_terms(rows_in, rows_grad, weight_gate, weight_up, weight_down):
    part_gate = jnp.dot(rows_in, weight_gate, preferred_element_type=jnp.float32)
    part_up = jnp.dot(rows_in, weight_up, preferred_element_type=jnp.float32)
    part_act = contract_cols(rows_grad, weight_down)
    pre_gate, pre_up, grad_act = lax.psum((part_gate, part_up, part_act), "dp")
    activated, grad_gate_pre, grad_up_pre = hidden_products(pre_gate, pre_up, grad_act)
    back = contract_cols(grad_gate_pre, weight_gate) + contract_cols(grad_up_pre, weight_up)
    return (
        contract_rows(rows_in, grad_gate_pre),
        contract_rows(rows_in, grad_up_pre),
        contract_rows(activated, rows_grad),
        back,
    )


def shards(
    tokens,
    grad_out,
    route_ids,
    route_gates,
    w_gate,
    w_up,
    w_down,
    shared_gate,
    shared_up,
    shared_down,
):
    n_exp = lax.axis_size("expert")
    capacity = CAP
    grad_scale = 1.0 / n_exp
    targets = jnp.arange(n_exp, dtype=jnp.int32)
    matches = route_ids[:, :, None] == targets[None, None, :]
    chosen = jnp.any(matches, axis=1).astype(jnp.int32)
    gate_total = jnp.sum(jnp.where(matches, route_gates[:, :, None], 0.0), axis=1)
    slot_rank = jnp.cumsum(chosen, axis=0) - 1
    slot_ids = jnp.arange(capacity, dtype=jnp.int32)
    placement = (chosen[:, :, None] == 1) & (slot_rank[:, :, None] == slot_ids[None, None, :])
    place_bf = placement.astype(jnp.bfloat16)
    send_in = jnp.einsum(
        "tec,td->ecd", place_bf, tokens, preferred_element_type=jnp.float32
    ).astype(jnp.bfloat16)
    slot_gate = jnp.einsum("tec,te->ec", placement.astype(jnp.float32), gate_total)
    picked_grad = jnp.einsum("tec,td->ecd", place_bf, grad_out, preferred_element_type=jnp.float32)
    send_grad = (slot_gate[:, :, None] * picked_grad).astype(jnp.bfloat16)
    recv_in = lax.all_to_all(send_in, "expert", split_axis=0, concat_axis=0, tiled=True)
    recv_grad = lax.all_to_all(send_grad, "expert", split_axis=0, concat_axis=0, tiled=True)
    width_dev = tokens.shape[1]
    rows_in = recv_in.reshape(n_exp * capacity, width_dev)
    rows_grad = recv_grad.reshape(n_exp * capacity, width_dev)
    part_gate, part_up, part_down, back = expert_terms(
        rows_in, rows_grad, w_gate[0], w_up[0], w_down[0]
    )
    grad_gate = (part_gate * grad_scale).astype(jnp.bfloat16)[None]
    grad_up = (part_up * grad_scale).astype(jnp.bfloat16)[None]
    grad_down = (part_down * grad_scale).astype(jnp.bfloat16)[None]
    back_rows = lax.all_to_all(
        back.astype(jnp.bfloat16).reshape(n_exp, capacity, width_dev),
        "expert",
        split_axis=0,
        concat_axis=0,
        tiled=True,
    )
    routed = jnp.einsum("tec,ecd->td", place_bf, back_rows, preferred_element_type=jnp.float32)
    whole_gate, whole_up, whole_down = (
        lax.all_gather(shared_gate, "expert", axis=1, tiled=True),
        lax.all_gather(shared_up, "expert", axis=1, tiled=True),
        lax.all_gather(shared_down, "expert", axis=0, tiled=True),
    )
    own_gate, own_up, own_down, shared_back = expert_terms(
        tokens, grad_out, whole_gate, whole_up, whole_down
    )
    sum_gate, sum_up, sum_down = (
        lax.psum_scatter(own_gate, "expert", scatter_dimension=1, tiled=True),
        lax.psum_scatter(own_up, "expert", scatter_dimension=1, tiled=True),
        lax.psum_scatter(own_down, "expert", scatter_dimension=0, tiled=True),
    )
    grad_tokens = (shared_back + routed).astype(jnp.bfloat16)
    return (
        grad_tokens,
        grad_gate,
        grad_up,
        grad_down,
        sum_gate * grad_scale,
        sum_up * grad_scale,
        sum_down * grad_scale,
    )


def solution(mesh):
    in_specs = (
        P("expert", "dp"),
        P("expert", "dp"),
        P("expert", None),
        P("expert", None),
        P("expert", "dp", None),
        P("expert", "dp", None),
        P("expert", None, "dp"),
        P("dp", "expert"),
        P("dp", "expert"),
        P("expert", "dp"),
    )
    out_specs = (
        P("expert", "dp"),
        P("expert", "dp", None),
        P("expert", "dp", None),
        P("expert", None, "dp"),
        P("dp", "expert"),
        P("dp", "expert"),
        P("expert", "dp"),
    )
    return jax.shard_map(shards, mesh=mesh, in_specs=in_specs, out_specs=out_specs, check_vma=False)
```

profile of v0, /device:TPU:0, one launch (start us, length us, event | category | flops | bytes accessed | tf_op | source)
XLA Modules:
  0.0 757.0 jit_solution(11704278710832089684)
XLA Ops:
  14.2 7.3 all-to-all-start
  22.5 23.6 %all-to-all-done = bf16[8,12,1792]{2,1,0:T(8,128)(2,1)S(1)} async-done(((bf16[8,12,1792]{2,1,0:T(8,128)(2,1)}), bf16[8,12,1792]{2,1,0:T(8,128)(2,1)S(1)}, u32[]{:S(2)}, u32[]{:S(2)}) %all-to-all-start) | async-done | bytes 344096 | tf_op jit(solution)/shard_map/all_to_all | solution.py:79
  46.1 4.4 all-to-all-start.1
  50.6 21.3 %all-to-all-done.1 = bf16[8,12,1792]{2,1,0:T(8,128)(2,1)S(1)} async-done(((bf16[8,12,1792]{2,1,0:T(8,128)(2,1)}), bf16[8,12,1792]{2,1,0:T(8,128)(2,1)S(1)}, u32[]{:S(2)}, u32[]{:S(2)}) %all-to-all-start.1) | async-done | bytes 344096 | tf_op jit(solution)/shard_map/all_to_all | solution.py:78
  72.0 3.7 fusion.2
  79.1 17.1 %all-gather.6.cloned.1.call-done = bf16[1792,1024]{1,0:T(8,128)(2,1)} async-done(((bf16[1792,128]{1,0:T(8,128)(2,1)}), bf16[1792,1024]{1,0:T(8,128)(2,1)}) %all-gather.6.cloned.1.call-update) | async-done | bytes 3670032 | tf_op jit(solution)/shard_map/all_gather | solution.py:99
  96.3 4.1 fusion.48
  100.4 67.2 %all-gather.8.cloned.1.call-done = bf16[1792,1024]{1,0:T(8,128)(2,1)} async-done(((bf16[1792,128]{1,0:T(8,128)(2,1)}), bf16[1792,1024]{1,0:T(8,128)(2,1)}) %all-gather.8.cloned.1.call-update) | async-done | bytes 3670032 | tf_op jit(solution)/shard_map/all_gather | solution.py:98
  167.6 4.1 fusion.49
  171.7 63.1 %all-gather.4.cloned.1.call-done = bf16[1024,1792]{1,0:T(8,128)(2,1)} async-done(((bf16[128,1792]{1,0:T(8,128)(2,1)}), bf16[1024,1792]{1,0:T(8,128)(2,1)}) %all-gather.4.cloned.1.call-update) | async-done | bytes 3670032 | tf_op jit(solution)/shard_map/all_gather | solution.py:100
  234.8 4.2 fusion.47
  239.0 87.0 %all-reduce.3.cloned.1.call-done = (f32[96,1024]{1,0:T(8,128)}, f32[96,1024]{1,0:T(8,128)}, f32[96,1024]{1,0:T(8,128)}, f32[256,1024]{1,0:T(8,128)}, f32[256,1024]{1,0:T(8,128)}, /*index=5*/f32[256,1024]{1,0:T(8,128)}) async-done(((f32[96,1024]{1,0:T(8,128)}, f32[96,1024]{1,0:T(8,128)}, f32[96,1024]{1,0:T(8,128)}, f32[256,1024]{1,0:T(8,128)}, f32[256,1024]{1,0:T(8,128)}, /*index=5*/f32[256,1024]{1,0:T(8,128)}), ...) | async-done | bytes 4325392 | tf_op jit(solution)/shard_map/psum | solution.py:38
  328.6 4.1 convolution_bitcast_fusion.1
  332.8 4.2 convolution_bitcast_fusion
  338.5 5.6 fusion.25
  345.5 3.3 fusion
  350.9 5.6 all-to-all-start.2
  356.5 3.0 fusion.12
  359.5 3.0 fusion.10
  362.5 3.0 fusion.11
  367.9 15.1 %all-to-all-done.2 = bf16[8,12,1792]{2,1,0:T(8,128)(2,1)S(1)} async-done(((bf16[8,12,1792]{2,1,0:T(8,128)(2,1)}), bf16[8,12,1792]{2,1,0:T(8,128)(2,1)S(1)}, u32[]{:S(2)}, u32[]{:S(2)}) %all-to-all-start.2) | async-done | bytes 344096 | tf_op jit(solution)/shard_map/all_to_all | solution.py:89
  387.9 89.5 %reduce-scatter.4.cloned.1.call-done = f32[1792,128]{0,1:T(8,128)} async-done(((f32[1792,1024]{0,1:T(8,128)}), f32[1792,128]{0,1:T(8,128)}) %reduce-scatter.4.cloned.1.call-update) | async-done | bytes 917520 | tf_op jit(solution)/shard_map/reduce_scatter | solution.py:106
  479.9 132.7 %reduce-scatter.6.cloned.1.call-done = f32[1792,128]{0,1:T(8,128)} async-done(((f32[1792,1024]{0,1:T(8,128)}), f32[1792,128]{0,1:T(8,128)}) %reduce-scatter.6.cloned.1.call-update) | async-done | bytes 917520 | tf_op jit(solution)/shard_map/reduce_scatter | solution.py:107
  615.1 132.9 %reduce-scatter.8.cloned.1.call-done = f32[128,1792]{1,0:T(8,128)} async-done(((f32[1024,1792]{1,0:T(8,128)}), f32[128,1792]{1,0:T(8,128)}) %reduce-scatter.8.cloned.1.call-update) | async-done | bytes 917520 | tf_op jit(solution)/shard_map/reduce_scatter | solution.py:108
  (73 shorter events, 33.8 us)
Async XLA Ops:
  7.2 14.3 %copy-start = (bf16[256,1792]{1,0:T(8,128)(2,1)S(1)}, bf16[256,1792]{1,0:T(8,128)(2,1)}, u32[]{:S(2)}) copy-start(bf16[256,1792]{1,0:T(8,128)(2,1)} %param.10) | copy-start | bytes 2752516
  7.2 89.1 %all-gather.6.cloned.1.call-start = ((), (), s32[]{:S(2)}) async-start(), calls=%async_computation.7 | async-start | bytes 4128768 | tf_op jit(solution)/shard_map/all_gather | solution.py:99
  7.9 159.6 %all-gather.8.cloned.1.call-start = ((), (), s32[]{:S(2)}) async-start(), calls=%async_computation.8 | async-start | bytes 4128768 | tf_op jit(solution)/shard_map/all_gather | solution.py:98
  8.7 226.1 %all-gather.4.cloned.1.call-start = ((), (), s32[]{:S(2)}) async-start(), calls=%async_computation.6 | async-start | bytes 4128768 | tf_op jit(solution)/shard_map/all_gather | solution.py:100
  14.2 31.9 %all-to-all-start = ((bf16[8,12,1792]{2,1,0:T(8,128)(2,1)}), bf16[8,12,1792]{2,1,0:T(8,128)(2,1)S(1)}, u32[]{:S(2)}, u32[]{:S(2)}) async-start(bf16[8,12,1792]{2,1,0:T(8,128)(2,1)} %fusion.18), calls=%async_computation | async-start | bytes 917504 | tf_op jit(solution)/shard_map/all_to_all | solution.py:79
  46.1 25.8 %all-to-all-start.1 = ((bf16[8,12,1792]{2,1,0:T(8,128)(2,1)}), bf16[8,12,1792]{2,1,0:T(8,128)(2,1)S(1)}, u32[]{:S(2)}, u32[]{:S(2)}) async-start(bf16[8,12,1792]{2,1,0:T(8,128)(2,1)} %convolution_convert_fusion), calls=%async_computation.1 | async-start | bytes 917504 | tf_op jit(solution)/shard_map/all_to_all | solution.py:78
  50.5 275.6 %all-reduce.3.cloned.1.call-start = ((), (), s32[]{:S(2)}) async-start(), calls=%async_computation.12 | async-start | bytes 8650752 | tf_op jit(solution)/shard_map/psum | solution.py:38
  72.0 3.7 copy-start.2
  72.0 5.1 copy-start.7
  100.4 134.4 %copy-start.5 = (bf16[256,1792]{1,0:T(8,128)(2,1)S(1)}, bf16[256,1792]{1,0:T(8,128)(2,1)}, u32[]{:S(2)}) copy-start(bf16[256,1792]{1,0:T(8,128)(2,1)} %param.11) | copy-start | bytes 2752516
  239.0 238.4 %reduce-scatter.4.cloned.1.call-start = ((), (), s32[]{:S(2)}) async-start(), calls=%async_computation.9 | async-start | bytes 8257536 | tf_op jit(solution)/shard_map/reduce_scatter | solution.py:106
  328.6 4.1 copy-start.9
  332.7 279.9 %reduce-scatter.6.cloned.1.call-start = ((), (), s32[]{:S(2)}) async-start(), calls=%async_computation.10 | async-start | bytes 8257536 | tf_op jit(solution)/shard_map/reduce_scatter | solution.py:107
  337.0 1.2 copy-start.4
  337.0 1.5 copy-start.6
  337.0 411.0 %reduce-scatter.8.cloned.1.call-start = ((), (), s32[]{:S(2)}) async-start(), calls=%async_computation.11 | async-start | bytes 8257536 | tf_op jit(solution)/shard_map/reduce_scatter | solution.py:108
  344.0 1.2 copy-start.14
  344.1 4.7 copy-start.3
  350.9 32.1 %all-to-all-start.2 = ((bf16[8,12,1792]{2,1,0:T(8,128)(2,1)}), bf16[8,12,1792]{2,1,0:T(8,128)(2,1)S(1)}, u32[]{:S(2)}, u32[]{:S(2)}) async-start(bf16[8,12,1792]{2,1,0:T(8,128)(2,1)} %reshape.49), calls=%async_computation.2 | async-start | bytes 917504 | tf_op jit(solution)/shard_map/all_to_all | solution.py:89
  359.5 6.0 copy-start.10
  359.5 6.0 copy-start.15
  383.0 2.2 copy-start.8
  383.0 2.8 copy-start.11
  477.4 272.8 %copy-start.1 = (bf16[256,1792]{1,0:T(8,128)(2,1)S(1)}, bf16[256,1792]{1,0:T(8,128)(2,1)}, u32[]{:S(2)}) copy-start(bf16[256,1792]{1,0:T(8,128)(2,1)} %param.10) | copy-start | bytes 2752516
  (2 other events, 2.1 us)
Sparse Core Ops, SparseCore 0:
  10.1 86.1 all-gather.5
  98.3 69.2 all-gather.7
  169.8 64.9 all-gather.3
  239.1 86.9 all-reduce.2
  332.9 144.4 reduce-scatter.3
  480.8 131.7 reduce-scatter.5
  616.2 131.7 reduce-scatter.7
where the time goes:
time: 758 us; the launch traced here: 757 us
  waiting for transfers between devices  652 us (86%)
  matrix products  55.3 us (7%)
  starting transfers between devices  17.7 us (2%)
  between operations  14.3 us (2%)
  other arithmetic  9.6 us (1%)
  local copies, waits for them, and re-layouts  8.51 us (1%)
    reduce_scatter x1, waiting for transfers between devices, shards(): lax.psum_scatter(own_down, 'expert', scatter_dimension=0, tiled=True)  133 us
    reduce_scatter x1, waiting for transfers between devices, shards(): lax.psum_scatter(own_up, 'expert', scatter_dimension=1, tiled=True)  133 us
    reduce_scatter x1, waiting for transfers between devices, shards(): lax.psum_scatter(own_gate, 'expert', scatter_dimension=1, tiled=True)  89.5 us
    psum x1, waiting for transfers between devices, expert_terms(): pre_gate, pre_up, grad_act = lax.psum((part_gate, part_up, part_act), 'dp')  87 us
    all_gather x1, waiting for transfers between devices, shards(): lax.all_gather(shared_gate, 'expert', axis=1, tiled=True)  67.2 us
    all_gather x1, waiting for transfers between devices, shards(): lax.all_gather(shared_down, 'expert', axis=0, tiled=True)  63.1 us
    all_to_all x1, waiting for transfers between devices, shards(): lax.all_to_all(send_grad, 'expert', split_axis=0, concat_axis=0, tiled=True)  23.6 us
    dot_general x6, matrix products, contract_rows(): lax.dot_general(left, right, (((0,), (0,)), ((), ())), preferred_element_...  22.8 us
  transfers between devices with their start and end apart: 10, of which 10 were waited for; matrix products, arithmetic and copies ran while one was open for 7% of the time, Pallas kernels for 0%

commit v1 on v0

--- a/solution.py
+++ b/solution.py
@@ -31,18 +31,32 @@
     return (activated, grad_gate_pre, grad_up_pre)
 
 
-def expert_terms(rows_in, rows_grad, weight_gate, weight_up, weight_down):
+def axis_groups(n_exp):
+    inner = 1
+    while inner * inner * 4 <= n_exp:
+        inner *= 2
+    outer = n_exp // inner
+    near = [[o * inner + i for i in range(inner)] for o in range(outer)]
+    far = [[o * inner + i for o in range(outer)] for i in range(inner)]
+    return near, far
+
+
+def partial_products(rows_in, rows_grad, weight_gate, weight_up, weight_down):
     part_gate = jnp.dot(rows_in, weight_gate, preferred_element_type=jnp.float32)
     part_up = jnp.dot(rows_in, weight_up, preferred_element_type=jnp.float32)
     part_act = contract_cols(rows_grad, weight_down)
-    pre_gate, pre_up, grad_act = lax.psum((part_gate, part_up, part_act), "dp")
+    return tuple(part.astype(jnp.bfloat16) for part in (part_gate, part_up, part_act))
+
+
+def expert_grads(sums, rows_in, rows_grad, weight_gate, weight_up):
+    pre_gate, pre_up, grad_act = (total.astype(jnp.float32) for total in sums)
     activated, grad_gate_pre, grad_up_pre = hidden_products(pre_gate, pre_up, grad_act)
     back = contract_cols(grad_gate_pre, weight_gate) + contract_cols(grad_up_pre, weight_up)
     return (
         contract_rows(rows_in, grad_gate_pre),
         contract_rows(rows_in, grad_up_pre),
         contract_rows(activated, rows_grad),
-        back,
+        back.astype(jnp.bfloat16),
     )
 
 
@@ -75,47 +89,51 @@
     slot_gate = jnp.einsum("tec,te->ec", placement.astype(jnp.float32), gate_total)
     picked_grad = jnp.einsum("tec,td->ecd", place_bf, grad_out, preferred_element_type=jnp.float32)
     send_grad = (slot_gate[:, :, None] * picked_grad).astype(jnp.bfloat16)
-    recv_in = lax.all_to_all(send_in, "expert", split_axis=0, concat_axis=0, tiled=True)
-    recv_grad = lax.all_to_all(send_grad, "expert", split_axis=0, concat_axis=0, tiled=True)
     width_dev = tokens.shape[1]
-    rows_in = recv_in.reshape(n_exp * capacity, width_dev)
-    rows_grad = recv_grad.reshape(n_exp * capacity, width_dev)
-    part_gate, part_up, part_down, back = expert_terms(
-        rows_in, rows_grad, w_gate[0], w_up[0], w_down[0]
+    near, far = axis_groups(n_exp)
+
+    def scatter(part, groups, dim):
+        return lax.psum_scatter(
+            part, "expert", scatter_dimension=dim, axis_index_groups=groups, tiled=True
+        )
+
+    def gather(part, groups, dim):
+        return lax.all_gather(part, "expert", axis=dim, axis_index_groups=groups, tiled=True)
+
+    recv = lax.all_to_all(
+        jnp.concatenate([send_in, send_grad], axis=1), "expert", split_axis=0, concat_axis=0, tiled=True
     )
-    grad_gate = (part_gate * grad_scale).astype(jnp.bfloat16)[None]
-    grad_up = (part_up * grad_scale).astype(jnp.bfloat16)[None]
-    grad_down = (part_down * grad_scale).astype(jnp.bfloat16)[None]
+    rows_in = recv[:, :capacity].reshape(n_exp * capacity, width_dev)
+    rows_grad = recv[:, capacity:].reshape(n_exp * capacity, width_dev)
+    all_in, all_grad = gather(tokens, near, 0), gather(grad_out, near, 0)
+    far_gate, far_up, far_down = (
+        gather(shared_gate, far, 1), gather(shared_up, far, 1), gather(shared_down, far, 0)
+    )
+    routed_parts = partial_products(rows_in, rows_grad, w_gate[0], w_up[0], w_down[0])
+    shared_parts = partial_products(all_in, all_grad, far_gate, far_up, far_down)
+    sums = lax.psum(routed_parts + shared_parts, "dp")
+    own_gate, own_up, own_down, shared_back = expert_grads(
+        sums[3:], all_in, all_grad, far_gate, far_up
+    )
+    part_gate, part_up, part_down, back = expert_grads(
+        sums[:3], rows_in, rows_grad, w_gate[0], w_up[0]
+    )
+    sum_gate = scatter(own_gate.astype(jnp.bfloat16), far, 1)
+    sum_up = scatter(own_up.astype(jnp.bfloat16), far, 1)
+    sum_down = scatter(own_down.astype(jnp.bfloat16), far, 0)
+    sum_back = scatter(shared_back, near, 0)
     back_rows = lax.all_to_all(
-        back.astype(jnp.bfloat16).reshape(n_exp, capacity, width_dev),
-        "expert",
-        split_axis=0,
-        concat_axis=0,
-        tiled=True,
+        back.reshape(n_exp, capacity, width_dev), "expert", split_axis=0, concat_axis=0, tiled=True
     )
     routed = jnp.einsum("tec,ecd->td", place_bf, back_rows, preferred_element_type=jnp.float32)
-    whole_gate, whole_up, whole_down = (
-        lax.all_gather(shared_gate, "expert", axis=1, tiled=True),
-        lax.all_gather(shared_up, "expert", axis=1, tiled=True),
-        lax.all_gather(shared_down, "expert", axis=0, tiled=True),
-    )
-    own_gate, own_up, own_down, shared_back = expert_terms(
-        tokens, grad_out, whole_gate, whole_up, whole_down
-    )
-    sum_gate, sum_up, sum_down = (
-        lax.psum_scatter(own_gate, "expert", scatter_dimension=1, tiled=True),
-        lax.psum_scatter(own_up, "expert", scatter_dimension=1, tiled=True),
-        lax.psum_scatter(own_down, "expert", scatter_dimension=0, tiled=True),
-    )
-    grad_tokens = (shared_back + routed).astype(jnp.bfloat16)
     return (
-        grad_tokens,
-        grad_gate,
-        grad_up,
-        grad_down,
-        sum_gate * grad_scale,
-        sum_up * grad_scale,
-        sum_down * grad_scale,
+        (sum_back.astype(jnp.float32) + routed).astype(jnp.bfloat16),
+        (part_gate * grad_scale).astype(jnp.bfloat16)[None],
+        (part_up * grad_scale).astype(jnp.bfloat16)[None],
+        (part_down * grad_scale).astype(jnp.bfloat16)[None],
+        sum_gate.astype(jnp.float32) * grad_scale,
+        sum_up.astype(jnp.float32) * grad_scale,
+        sum_down.astype(jnp.float32) * grad_scale,
     )
 
 

time: 758 us -> 437 us (0.58)
  waiting for transfers between devices: 652 us -> 341 us
    reduce_scatter x3 -> x4, waiting for transfers between devices: 355 us -> 114 us  [scatter(): lax.psum_scatter(part, 'expert', scatter_dimension=dim, axis_index_groups...]
    all_to_all x3 -> x2, waiting for transfers between devices: 60 us -> 17.4 us  [the longest x1 17.4 us: shards(): lax.all_to_all(jnp.concatenate([send_in, send_grad], axis=1), 'expert', s...]
    psum x1, waiting for transfers between devices: 87 us -> 52.3 us  [shards(): sums = lax.psum(routed_parts + shared_parts, 'dp')]
    all_gather x3 -> x5, waiting for transfers between devices: 147 us -> 154 us  [gather(): lax.all_gather(part, 'expert', axis=dim, axis_index_groups=groups, tiled=...]
    all_to_all x3 -> x2, starting transfers between devices: 17.2 us -> 13 us  [the longest x1 7.28 us: shards(): lax.all_to_all(jnp.concatenate([send_in, send_grad], axis=1), 'expert', s...]
  transfers between devices with their start and end apart: 10 -> 12, of which waited for: 10 -> 11; matrix products, arithmetic and copies ran while one was open for 7% -> 12% of each run, Pallas kernels for 0% -> 0%
where the time goes in v1:
time: 437 us
  waiting for transfers between devices  341 us (78%)
  matrix products  52.1 us (12%)
  between operations  14.4 us (3%)
  starting transfers between devices  13.5 us (3%)
  local copies, waits for them, and re-layouts  9.26 us (2%)
  other arithmetic  5.91 us (1%)
    all_gather x5, waiting for transfers between devices, gather(): lax.all_gather(part, 'expert', axis=dim, axis_index_groups=groups, tiled=...  154 us
    reduce_scatter x4, waiting for transfers between devices, scatter(): lax.psum_scatter(part, 'expert', scatter_dimension=dim, axis_index_groups...  114 us
    psum x1, waiting for transfers between devices, shards(): sums = lax.psum(routed_parts + shared_parts, 'dp')  52.3 us
    dot_general x6, matrix products, contract_rows(): lax.dot_general(left, right, (((0,), (0,)), ((), ())), preferred_element_...  20.3 us
    all_to_all x1, waiting for transfers between devices, shards(): lax.all_to_all(jnp.concatenate([send_in, send_grad], axis=1), 'expert', s...  17.4 us
    dot_general x6, matrix products, contract_cols(): lax.dot_general(left, right, (((1,), (1,)), ((), ())), preferred_element_...  16.2 us
  transfers between devices with their start and end apart: 12, of which 11 were waited for; matrix products, arithmetic and copies ran while one was open for 12% of the time, Pallas kernels for 0%

profile of v1, /device:TPU:0, one launch (start us, length us, event | category | flops | bytes accessed | tf_op | source)
XLA Modules:
  0.0 436.7 jit_solution(9072068373334029075)
XLA Ops:
  12.8 7.3 %all-to-all-start = ((bf16[8,24,1792]{2,1,0:T(8,128)(2,1)}), bf16[8,24,1792]{2,1,0:T(8,128)(2,1)S(1)}, u32[]{:S(2)}, u32[]{:S(2)}) async-start(bf16[8,24,1792]{2,1,0:T(8,128)(2,1)} %pad_maximum_fusion), calls=%async_computation.1 | async-start | bytes 1376256 | tf_op jit(solution)/shard_map/all_to_all | solution.py:103
  20.7 17.4 %all-to-all-done = bf16[8,24,1792]{2,1,0:T(8,128)(2,1)S(1)} async-done(((bf16[8,24,1792]{2,1,0:T(8,128)(2,1)}), bf16[8,24,1792]{2,1,0:T(8,128)(2,1)S(1)}, u32[]{:S(2)}, u32[]{:S(2)}) %all-to-all-start) | async-done | bytes 688160 | tf_op jit(solution)/shard_map/all_to_all | solution.py:103
  38.4 3.6 fusion.30
  46.0 3.7 all-gather.10.cloned.1.call-done
  49.7 43.5 %all-gather.14.cloned.1.call-done = bf16[1792,512]{1,0:T(8,128)(2,1)} async-done(((bf16[1792,128]{1,0:T(8,128)(2,1)}), bf16[1792,512]{1,0:T(8,128)(2,1)}) %all-gather.14.cloned.1.call-update) | async-done | bytes 1835024 | tf_op jit(solution)/shard_map/all_gather | solution.py:101
  93.2 4.0 convolution_convert_fusion.4
  97.2 37.9 %all-gather.12.cloned.1.call-done = bf16[1792,512]{1,0:T(8,128)(2,1)} async-done(((bf16[1792,128]{1,0:T(8,128)(2,1)}), bf16[1792,512]{1,0:T(8,128)(2,1)}) %all-gather.12.cloned.1.call-update) | async-done | bytes 1835024 | tf_op jit(solution)/shard_map/all_gather | solution.py:101
  135.0 3.4 convolution_convert_fusion.5
  138.4 26.4 %all-gather.6.cloned.1.call-done = bf16[512,1792]{1,0:T(8,128)(2,1)} async-done(((bf16[256,1792]{1,0:T(8,128)(2,1)}), bf16[512,1792]{1,0:T(8,128)(2,1)}) %all-gather.6.cloned.1.call-update) | async-done | bytes 1835024 | tf_op jit(solution)/shard_map/all_gather | solution.py:101
  164.9 42.8 %all-gather.8.cloned.1.call-done = bf16[512,1792]{1,0:T(8,128)(2,1)} async-done(((bf16[128,1792]{1,0:T(8,128)(2,1)}), bf16[512,1792]{1,0:T(8,128)(2,1)}) %all-gather.8.cloned.1.call-update) | async-done | bytes 1835024 | tf_op jit(solution)/shard_map/all_gather | solution.py:101
  207.7 4.0 convolution_convert_fusion.6
  211.8 52.3 %all-reduce.3.cloned.1.call-done = (bf16[96,1024]{1,0:T(8,128)(2,1)}, bf16[96,1024]{1,0:T(8,128)(2,1)}, bf16[96,1024]{1,0:T(8,128)(2,1)}, bf16[512,512]{1,0:T(8,...) async-done(((bf16[96,1024]{1,0:T(8,128)(2,1)}, bf16[96,1024]{1,0:T(8,128)(2,1)}, bf16[96,1024]{1,0:T(8,128)(2,1)}, bf16[512,512]{1,0:T(8,128)(2,1)}, ...) | async-done | bytes 2162704 | tf_op jit(solution)/shard_map/psum | solution.py:114
  264.1 4.0 fusion.13
  269.1 3.5 fusion.14
  274.2 3.8 convolution_convert_fusion
  286.1 3.5 fusion
  291.7 5.7 %all-to-all-start.1 = ((bf16[8,12,1792]{2,1,0:T(8,128)(2,1)}), bf16[8,12,1792]{2,1,0:T(8,128)(2,1)S(1)}, u32[]{:S(2)}, u32[]{:S(2)}) async-start(bf16[8,12,1792]{2,1,0:T(8,128)(2,1)} %reshape.49), calls=%async_computation.2 | async-start | bytes 917504 | tf_op jit(solution)/shard_map/all_to_all | solution.py:125
  297.4 3.0 fusion.12
  300.4 3.0 fusion.11
  303.4 3.0 fusion.10
  306.4 6.4 %reduce-scatter.7.cloned.1.call-done = bf16[1792,128]{0,1:T(8,128)(2,1)} async-done(((bf16[1792,512]{0,1:T(8,128)(2,1)}), bf16[1792,128]{0,1:T(8,128)(2,1)}) %reduce-scatter.7.cloned.1.call-update) | async-done | bytes 458768 | tf_op jit(solution)/shard_map/reduce_scatter | solution.py:96
  313.9 42.1 %reduce-scatter.9.cloned.1.call-done = bf16[1792,128]{0,1:T(8,128)(2,1)} async-done(((bf16[1792,512]{0,1:T(8,128)(2,1)}), bf16[1792,128]{0,1:T(8,128)(2,1)}) %reduce-scatter.9.cloned.1.call-update) | async-done | bytes 458768 | tf_op jit(solution)/shard_map/reduce_scatter | solution.py:96
  359.5 37.5 %reduce-scatter.11.cloned.1.call-done = bf16[128,1792]{1,0:T(8,128)(2,1)} async-done(((bf16[512,1792]{1,0:T(8,128)(2,1)}), bf16[128,1792]{1,0:T(8,128)(2,1)}) %reduce-scatter.11.cloned.1.call-update) | async-done | bytes 458768 | tf_op jit(solution)/shard_map/reduce_scatter | solution.py:96
  399.0 28.3 %reduce-scatter.5.cloned.1.call-done = bf16[256,1792]{1,0:T(8,128)(2,1)} async-done(((bf16[512,1792]{1,0:T(8,128)(2,1)}), bf16[256,1792]{1,0:T(8,128)(2,1)}) %reduce-scatter.5.cloned.1.call-update) | async-done | bytes 917520 | tf_op jit(solution)/shard_map/reduce_scatter | solution.py:96
  (80 shorter events, 32.3 us)
Async XLA Ops:
  7.2 4.0 copy-start
  7.2 2.8 copy-start.5
  7.2 2.8 copy-start.6
  7.2 42.5 %all-gather.10.cloned.1.call-start = ((), (), s32[]{:S(2)}) async-start(), calls=%async_computation.8 | async-start | bytes 2752512 | tf_op jit(solution)/shard_map/all_gather | solution.py:101
  7.9 3.5 copy-start.1
  7.9 85.3 %all-gather.14.cloned.1.call-start = ((), (), s32[]{:S(2)}) async-start(), calls=%async_computation.10 | async-start | bytes 2293760 | tf_op jit(solution)/shard_map/all_gather | solution.py:101
  8.7 126.3 %all-gather.12.cloned.1.call-start = ((), (), s32[]{:S(2)}) async-start(), calls=%async_computation.9 | async-start | bytes 2293760 | tf_op jit(solution)/shard_map/all_gather | solution.py:101
  9.4 155.4 %all-gather.6.cloned.1.call-start = ((), (), s32[]{:S(2)}) async-start(), calls=%async_computation.6 | async-start | bytes 2752512 | tf_op jit(solution)/shard_map/all_gather | solution.py:101
  12.8 25.3 %all-to-all-start = ((bf16[8,24,1792]{2,1,0:T(8,128)(2,1)}), bf16[8,24,1792]{2,1,0:T(8,128)(2,1)S(1)}, u32[]{:S(2)}, u32[]{:S(2)}) async-start(bf16[8,24,1792]{2,1,0:T(8,128)(2,1)} %pad_maximum_fusion), calls=%async_computation.1 | async-start | bytes 1376256 | tf_op jit(solution)/shard_map/all_to_all | solution.py:103
  20.1 187.6 %all-gather.8.cloned.1.call-start = ((), (), s32[]{:S(2)}) async-start(), calls=%async_computation.7 | async-start | bytes 2293760 | tf_op jit(solution)/shard_map/all_gather | solution.py:101
  20.7 243.5 %all-reduce.3.cloned.1.call-start = ((), (), s32[]{:S(2)}) async-start(), calls=%async_computation.15 | async-start | bytes 4325376 | tf_op jit(solution)/shard_map/psum | solution.py:114
  38.4 3.6 copy-start.3
  42.0 2.1 copy-start.2
  49.7 85.3 %copy-start.9 = (bf16[512,1792]{1,0:T(8,128)(2,1)S(1)}, bf16[512,1792]{1,0:T(8,128)(2,1)}, u32[]{:S(2)}) copy-start(bf16[512,1792]{1,0:T(8,128)(2,1)} %all-gather.10.cloned.1.call-done) | copy-start | bytes 5505028
  211.7 101.1 %reduce-scatter.7.cloned.1.call-start = ((), (), s32[]{:S(2)}) async-start(), calls=%async_computation.12 | async-start | bytes 2293760 | tf_op jit(solution)/shard_map/reduce_scatter | solution.py:96
  268.1 87.8 %reduce-scatter.9.cloned.1.call-start = ((), (), s32[]{:S(2)}) async-start(), calls=%async_computation.13 | async-start | bytes 2293760 | tf_op jit(solution)/shard_map/reduce_scatter | solution.py:96
  272.7 1.5 copy-start.10
  272.7 124.3 %reduce-scatter.11.cloned.1.call-start = ((), (), s32[]{:S(2)}) async-start(), calls=%async_computation.14 | async-start | bytes 2293760 | tf_op jit(solution)/shard_map/reduce_scatter | solution.py:96
  277.9 1.5 copy-start.7
  278.0 149.3 %reduce-scatter.5.cloned.1.call-start = ((), (), s32[]{:S(2)}) async-start(), calls=%async_computation.11 | async-start | bytes 2752512 | tf_op jit(solution)/shard_map/reduce_scatter | solution.py:96
  279.4 2.9 copy-start.8
  279.4 2.9 copy-start.12
  286.1 3.5 copy-start.4
  291.7 107.3 %all-to-all-start.1 = ((bf16[8,12,1792]{2,1,0:T(8,128)(2,1)}), bf16[8,12,1792]{2,1,0:T(8,128)(2,1)S(1)}, u32[]{:S(2)}, u32[]{:S(2)}) async-start(bf16[8,12,1792]{2,1,0:T(8,128)(2,1)} %reshape.49), calls=%async_computation.2 | async-start | bytes 917504 | tf_op jit(solution)/shard_map/all_to_all | solution.py:125
  (4 other events, 4.1 us)
Sparse Core Ops, SparseCore 0:
  9.6 40.0 all-gather.9
  51.3 41.9 all-gather.13
  94.8 40.1 all-gather.11
  136.4 28.3 all-gather.5
  166.3 41.3 all-gather.7
  211.8 52.2 all-reduce.2
  268.2 44.4 reduce-scatter.6
  315.2 40.7 reduce-scatter.8
  358.4 38.5 reduce-scatter.10
  399.2 28.0 reduce-scatter.4

commit v2 on v0

v2 whole, which is shorter than its diff:
```python
import functools

import jax
import jax.numpy as jnp
from jax import lax
from jax.experimental import pallas as pl
from jax.experimental.pallas import tpu as pltpu
from jax.sharding import PartitionSpec as P

CAP = 12
SLOT = 16
NEAR = 4
MESH = pl.DeviceIdType.MESH
ANY = pl.BlockSpec(memory_space=pl.ANY)
VMEM = pl.BlockSpec(memory_space=pltpu.VMEM)


def silu_parts(pre):
    sigmoid_val = jax.nn.sigmoid(pre)
    return (pre * sigmoid_val, sigmoid_val * (1.0 + pre * (1.0 - sigmoid_val)))


def contract_rows(left, right):
    return lax.dot_general(
        left, right, (((0,), (0,)), ((), ())), preferred_element_type=jnp.float32
    )


def contract_cols(left, right):
    return lax.dot_general(
        left, right, (((1,), (1,)), ((), ())), preferred_element_type=jnp.float32
    )


def hidden_products(part_gate, part_up, part_act):
    silu_val, silu_slope = silu_parts(part_gate)
    activated = (silu_val * part_up).astype(jnp.bfloat16)
    grad_gate_pre = (part_act * part_up * silu_slope).astype(jnp.bfloat16)
    grad_up_pre = (part_act * silu_val).astype(jnp.bfloat16)
    return (activated, grad_gate_pre, grad_up_pre)


def greet(peers):
    barrier = pltpu.get_barrier_semaphore()
    for peer in peers:
        pl.semaphore_signal(barrier, inc=1, device_id=peer, device_id_type=MESH)
    pl.semaphore_wait(barrier, len(peers))


def remote(src, dst, sems, k, peer):
    return pltpu.make_async_remote_copy(
        src_ref=src,
        dst_ref=dst,
        send_sem=sems[0].at[k],
        recv_sem=sems[1].at[k],
        device_id=peer,
        device_id_type=MESH,
    )


def expert_peers(n_exp):
    dp, me = lax.axis_index("dp"), lax.axis_index("expert")
    far, near = me // NEAR, me % NEAR
    high, low = near // 2, near % 2
    n_far = n_exp // NEAR
    base = far * NEAR
    across = (dp, base + (1 - high) * 2 + low)
    beside = (dp, base + high * 2 + 1 - low)
    corner = (dp, base + (1 - high) * 2 + 1 - low)
    distant = [(dp, lax.rem(far + k, n_far) * NEAR + near) for k in range(1, n_far)]
    every = [(dp, lax.rem(me + k, n_exp)) for k in range(1, n_exp)]
    return me, near, far, across, beside, corner, distant, every


def gather_kernel(n_exp, *refs):
    tokens, grads, *weights = refs[:5]
    sends = refs[5]
    all_tokens, all_grads, *all_weights = refs[6:11]
    recv = refs[11]
    near_sems, far_sems, route_sems = refs[12:14], refs[14:16], refs[16:18]
    own_sem = refs[18]
    me, near, far, across, beside, corner, distant, every = expert_peers(n_exp)
    greet(every)
    pairs = ((tokens, all_tokens), (grads, all_grads))
    copies, relays = [], []
    for k, (src, dst) in enumerate(pairs):
        relays.append(remote(src, dst.at[near], near_sems, 3 * k, across))
        copies.append(remote(src, dst.at[near], near_sems, 3 * k + 1, beside))
        relays[-1].start()
        copies[-1].start()
    for k, peer in enumerate(every):
        copies.append(remote(sends.at[peer[1]], recv.at[me], route_sems, k, peer))
        copies[-1].start()
    for k, peer in enumerate(distant):
        for w in range(3):
            copies.append(remote(weights[w], all_weights[w].at[far], far_sems, 3 * k + w, peer))
            copies[-1].start()
    own = [
        pltpu.make_async_copy(src, dst, own_sem.at[k])
        for k, (src, dst) in enumerate(
            [(src, dst.at[near]) for src, dst in pairs]
            + [(weights[w], all_weights[w].at[far]) for w in range(3)]
            + [(sends.at[me], recv.at[me])]
        )
    ]
    for copy in own:
        copy.start()
    other = lax.rem(near + 2, NEAR)
    for k, (_, dst) in enumerate(pairs):
        relays[k].wait_recv()
        copies.append(remote(dst.at[other], dst.at[other], near_sems, 3 * k + 2, beside))
        copies[-1].start()
    for copy in relays:
        copy.wait_send()
    for copy in own:
        copy.wait()
    for copy in copies:
        copy.wait()


def gather_call(n_exp, *args):
    n_far = n_exp // NEAR
    shapes = [(NEAR,) + a.shape for a in args[:2]] + [(n_far,) + a.shape for a in args[2:5]]
    shapes.append(args[5].shape)
    counts = (6, 6, 3 * (n_far - 1), 3 * (n_far - 1), n_exp - 1, n_exp - 1, 6)
    return pl.pallas_call(
        functools.partial(gather_kernel, n_exp),
        out_shape=[jax.ShapeDtypeStruct(shape, jnp.bfloat16) for shape in shapes],
        in_specs=[ANY] * 6,
        out_specs=[ANY] * 6,
        scratch_shapes=[pltpu.SemaphoreType.DMA((count,)) for count in counts],
        compiler_params=pltpu.CompilerParams(collective_id=1, has_side_effects=True),
    )(*args)


def scatter_kernel(n_exp, *refs):
    back, *parts = refs[:4]
    sends = refs[4]
    got_back, *got_parts = refs[5:9]
    recv = refs[9]
    near_sems, far_sems, route_sems = refs[10:12], refs[12:14], refs[14:16]
    own_sem = refs[16]
    me, near, far, across, beside, corner, distant, every = expert_peers(n_exp)
    greet(every)
    copies = []
    for k, peer in enumerate(distant):
        for w in range(3):
            copies.append(
                remote(parts[w].at[peer[1] // NEAR], got_parts[w].at[far], far_sems, 3 * k + w, peer)
            )
    for k, peer in enumerate((corner, across, beside)):
        copies.append(remote(back.at[lax.rem(peer[1], NEAR)], got_back.at[near], near_sems, k, peer))
    for k, peer in enumerate(every):
        copies.append(remote(sends.at[peer[1]], recv.at[me], route_sems, k, peer))
    own = [
        pltpu.make_async_copy(src, dst, own_sem.at[k])
        for k, (src, dst) in enumerate(
            [(back.at[near], got_back.at[near])]
            + [(parts[w].at[far], got_parts[w].at[far]) for w in range(3)]
            + [(sends.at[me], recv.at[me])]
        )
    ]
    for copy in copies + own:
        copy.start()
    for copy in own + copies:
        copy.wait()


def scatter_call(n_exp, *args):
    n_far = n_exp // NEAR
    counts = (3, 3, 3 * (n_far - 1), 3 * (n_far - 1), n_exp - 1, n_exp - 1, 5)
    return pl.pallas_call(
        functools.partial(scatter_kernel, n_exp),
        out_shape=[jax.ShapeDtypeStruct(a.shape, jnp.bfloat16) for a in args],
        in_specs=[ANY] * 5,
        out_specs=[ANY] * 5,
        scratch_shapes=[pltpu.SemaphoreType.DMA((count,)) for count in counts],
        compiler_params=pltpu.CompilerParams(collective_id=2, has_side_effects=True),
    )(*args)


def hidden_kernel(n_dp, *refs):
    parts, outs = refs[:2], refs[2:4]
    met, held, far = refs[4:6], refs[6:8], refs[8:10]
    meet_sems, far_sems, give_sems = refs[10:12], refs[12:14], refs[14:16]
    dp, expert = lax.axis_index("dp"), lax.axis_index("expert")
    chip, core = dp // 2, dp % 2
    chips = n_dp // 2
    twin = (chip * 2 + 1 - core, expert)
    peers = [(lax.rem(chip + k, chips) * 2 + core, expert) for k in range(1, chips)]
    greet([twin] + peers)
    meets = [remote(parts[a].at[:, 1 - core], met[a], meet_sems, a, twin) for a in range(2)]
    for copy in meets:
        copy.start()
    copies = []
    for a in range(2):
        rows = 64 if met[a].shape[1] % 64 == 0 else SLOT
        meets[a].wait()

        @pl.loop(0, met[a].shape[1] // rows)
        def _(step):
            at = pl.ds(pl.multiple_of(step * rows, rows), rows)
            for w in range(3):
                held[a][w, at] = (
                    parts[a][w, core, at].astype(jnp.float32) + met[a][w, at].astype(jnp.float32)
                ).astype(jnp.bfloat16)

        copies.append(
            [
                remote(held[a], far[a].at[k], far_sems, a * (chips - 1) + k, peer)
                for k, peer in enumerate(peers)
            ]
        )
        for copy in copies[-1]:
            copy.start()
    gives = []
    for a in range(2):
        rows = 64 if met[a].shape[1] % 64 == 0 else SLOT
        for copy in copies[a]:
            copy.wait()

        @pl.loop(0, met[a].shape[1] // rows)
        def _(step):
            at = pl.ds(pl.multiple_of(step * rows, rows), rows)
            totals = []
            for w in range(3):
                total = held[a][w, at].astype(jnp.float32)
                for k in range(chips - 1):
                    total = total + far[a][k, w, at].astype(jnp.float32)
                totals.append(total)
            for w, value in enumerate(hidden_products(*totals)):
                outs[a][w, core, at] = value

        gives.append(remote(outs[a].at[:, core], outs[a].at[:, core], give_sems, a, twin))
        gives[-1].start()
    for copy in gives:
        copy.wait()


def hidden_call(n_dp, *args):
    chips = n_dp // 2
    halves = [(3,) + a.shape[2:] for a in args]
    return pl.pallas_call(
        functools.partial(hidden_kernel, n_dp),
        out_shape=[jax.ShapeDtypeStruct(a.shape, jnp.bfloat16) for a in args],
        in_specs=[VMEM] * 2,
        out_specs=[VMEM] * 2,
        scratch_shapes=[pltpu.VMEM(shape, jnp.bfloat16) for shape in halves * 2]
        + [pltpu.VMEM((chips - 1,) + shape, jnp.bfloat16) for shape in halves]
        + [
            pltpu.SemaphoreType.DMA((count,))
            for count in (2, 2, 2 * (chips - 1), 2 * (chips - 1), 2, 2)
        ],
        compiler_params=pltpu.CompilerParams(
            collective_id=3, has_side_effects=True, vmem_limit_bytes=40 * 2**20
        ),
    )(*args)


def partial_products(rows_in, rows_grad, weight_gate, weight_up, weight_down):
    part_gate = jnp.dot(rows_in, weight_gate, preferred_element_type=jnp.float32)
    part_up = jnp.dot(rows_in, weight_up, preferred_element_type=jnp.float32)
    part_act = contract_cols(rows_grad, weight_down)
    parts = jnp.stack([part.astype(jnp.bfloat16) for part in (part_gate, part_up, part_act)])
    rows, width = part_gate.shape
    return parts.reshape(3, 2, rows // 2, width)


def shards(
    tokens,
    grad_out,
    route_ids,
    route_gates,
    w_gate,
    w_up,
    w_down,
    shared_gate,
    shared_up,
    shared_down,
):
    n_exp = lax.axis_size("expert")
    capacity = SLOT
    grad_scale = 1.0 / n_exp
    targets = jnp.arange(n_exp, dtype=jnp.int32)
    matches = route_ids[:, :, None] == targets[None, None, :]
    chosen = jnp.any(matches, axis=1).astype(jnp.int32)
    gate_total = jnp.sum(jnp.where(matches, route_gates[:, :, None], 0.0), axis=1)
    slot_rank = jnp.cumsum(chosen, axis=0) - 1
    slot_ids = jnp.arange(capacity, dtype=jnp.int32)
    placement = (chosen[:, :, None] == 1) & (slot_rank[:, :, None] == slot_ids[None, None, :])
    place_bf = placement.astype(jnp.bfloat16)
    picked_in = jnp.einsum("tec,td->ecd", place_bf, tokens, preferred_element_type=jnp.float32)
    slot_gate = jnp.einsum("tec,te->ec", placement.astype(jnp.float32), gate_total)
    picked_grad = jnp.einsum("tec,td->ecd", place_bf, grad_out, preferred_element_type=jnp.float32)
    picked = jnp.stack([picked_in, slot_gate[:, :, None] * picked_grad], axis=1).astype(jnp.bfloat16)
    width_dev = tokens.shape[1]
    sends = picked.reshape(n_exp, 2 * capacity, width_dev)
    all_in, all_grad, far_gate, far_up, far_down, recv = gather_call(
        n_exp, tokens, grad_out, shared_gate, shared_up, shared_down, sends
    )
    n_far = n_exp // NEAR
    width_sh = shared_gate.shape[1]
    all_in, all_grad = all_in.reshape(-1, width_dev), all_grad.reshape(-1, width_dev)
    far_gate = jnp.concatenate([far_gate[k] for k in range(n_far)], axis=1)
    far_up = jnp.concatenate([far_up[k] for k in range(n_far)], axis=1)
    far_down = far_down.reshape(-1, width_dev)
    recv = recv.reshape(n_exp, 2, capacity, width_dev)
    rows_in = recv[:, 0].reshape(n_exp * capacity, width_dev)
    rows_grad = recv[:, 1].reshape(n_exp * capacity, width_dev)
    shared_acts, routed_acts = hidden_call(
        lax.axis_size("dp"),
        partial_products(all_in, all_grad, far_gate, far_up, far_down),
        partial_products(rows_in, rows_grad, w_gate[0], w_up[0], w_down[0]),
    )
    act, grad_gate_pre, grad_up_pre = (
        shared_acts[w].reshape(-1, n_far * width_sh) for w in range(3)
    )
    back = contract_cols(grad_gate_pre, far_gate) + contract_cols(grad_up_pre, far_up)

    def own_columns(grad_pre):
        return jnp.stack(
            [
                contract_rows(all_in, grad_pre[:, k * width_sh : (k + 1) * width_sh])
                for k in range(n_far)
            ]
        ).astype(jnp.bfloat16)

    routed_act, routed_gate, routed_up = (
        routed_acts[w].reshape(n_exp * capacity, -1) for w in range(3)
    )
    route_back = contract_cols(routed_gate, w_gate[0]) + contract_cols(routed_up, w_up[0])
    got_back, got_gate, got_up, got_down, back_rows = scatter_call(
        n_exp,
        back.astype(jnp.bfloat16).reshape(NEAR, -1, width_dev),
        own_columns(grad_gate_pre),
        own_columns(grad_up_pre),
        contract_rows(act, all_grad).astype(jnp.bfloat16).reshape(n_far, width_sh, width_dev),
        route_back.astype(jnp.bfloat16).reshape(n_exp, capacity, width_dev),
    )

    def total(parts):
        return jnp.sum(parts.astype(jnp.float32), axis=0)

    routed = jnp.einsum("tec,ecd->td", place_bf, back_rows, preferred_element_type=jnp.float32)
    return (
        (total(got_back) + routed).astype(jnp.bfloat16),
        (contract_rows(rows_in, routed_gate) * grad_scale).astype(jnp.bfloat16)[None],
        (contract_rows(rows_in, routed_up) * grad_scale).astype(jnp.bfloat16)[None],
        (contract_rows(routed_act, rows_grad) * grad_scale).astype(jnp.bfloat16)[None],
        total(got_gate) * grad_scale,
        total(got_up) * grad_scale,
        total(got_down) * grad_scale,
    )


def solution(mesh):
    in_specs = (
        P("expert", "dp"),
        P("expert", "dp"),
        P("expert", None),
        P("expert", None),
        P("expert", "dp", None),
        P("expert", "dp", None),
        P("expert", None, "dp"),
        P("dp", "expert"),
        P("dp", "expert"),
        P("expert", "dp"),
    )
    out_specs = (
        P("expert", "dp"),
        P("expert", "dp", None),
        P("expert", "dp", None),
        P("expert", None, "dp"),
        P("dp", "expert"),
        P("dp", "expert"),
        P("expert", "dp"),
    )
    return jax.shard_map(shards, mesh=mesh, in_specs=in_specs, out_specs=out_specs, check_vma=False)
```

time: 758 us -> 277 us (0.37)
  waiting for transfers between devices: 652 us -> 0 us
  Pallas kernels: 0 us -> 223 us
  matrix products: 55.3 us -> 36.1 us
  starting transfers between devices: 17.7 us -> 0 us
  between operations: 14.3 us -> 0.95 us
    reduce_scatter x3 -> x0, waiting for transfers between devices: 355 us -> none  [the longest x1 133 us: shards(): lax.psum_scatter(own_down, 'expert', scatter_dimension=0, tiled=True)]
    pallas_call x0 -> x3, Pallas kernels: none -> 223 us  [the longest x1 110 us: gather_call(): pl.pallas_call(functools.partial(gather_kernel, n_exp), out_shape=[jax.Sh...]
    all_gather x3 -> x0, waiting for transfers between devices: 147 us -> none  [the longest x1 67.2 us: shards(): lax.all_gather(shared_gate, 'expert', axis=1, tiled=True)]
    psum x1 -> x0, waiting for transfers between devices: 87 us -> none  [expert_terms(): pre_gate, pre_up, grad_act = lax.psum((part_gate, part_up, part_act), 'dp')]
    all_to_all x3 -> x0, waiting for transfers between devices: 60 us -> none  [the longest x1 23.6 us: shards(): lax.all_to_all(send_grad, 'expert', split_axis=0, concat_axis=0, tiled=True)]
    all_to_all x3 -> x0, starting transfers between devices: 17.2 us -> none  [the longest x1 7.28 us: shards(): lax.all_to_all(send_grad, 'expert', split_axis=0, concat_axis=0, tiled=True)]
    dot_general x4, matrix products: 13.4 us -> 5.71 us  [the longest x2 3.95 us: partial_products(): jnp.dot(rows_in, weight_gate, preferred_element_type=jnp.float32)]
    dot_general x6 -> x8, matrix products: 22.8 us -> 15.9 us  [contract_rows(): lax.dot_general(left, right, (((0,), (0,)), ((), ())), preferred_element_...]
  transfers between devices with their start and end apart: 10 -> 0, of which waited for: 10 -> 0; matrix products, arithmetic and copies ran while one was open for 7% -> 0% of each run, Pallas kernels for 0% -> 0%
where the time goes in v2:
time: 277 us
  Pallas kernels  223 us (81%)
  matrix products  36.1 us (13%)
  other arithmetic  10.7 us (4%)
  local copies, waits for them, and re-layouts  6.5 us (2%)
    pallas_call x1, Pallas kernels, gather_call(): pl.pallas_call(functools.partial(gather_kernel, n_exp), out_shape=[jax.Sh...  110 us
    pallas_call x1, Pallas kernels, scatter_call(): pl.pallas_call(functools.partial(scatter_kernel, n_exp), out_shape=[jax.S...  80.1 us
    pallas_call x1, Pallas kernels, hidden_call(): pl.pallas_call(functools.partial(hidden_kernel, n_dp), out_shape=[jax.Sha...  32.4 us
    dot_general x8, matrix products, contract_rows(): lax.dot_general(left, right, (((0,), (0,)), ((), ())), preferred_element_...  15.9 us
    dot_general x6, matrix products, contract_cols(): lax.dot_general(left, right, (((1,), (1,)), ((), ())), preferred_element_...  10 us

profile of v2, /device:TPU:0, one launch (start us, length us, event | category | flops | bytes accessed | tf_op | source)
XLA Modules:
  0.0 276.8 jit_solution(7072778725094448864)
XLA Ops:
  3.2 1.5 fusion.22
  4.6 1.5 fusion.27
  7.2 110.1 %shard_map.153 = (bf16[4,256,1792]{2,1,0:T(8,128)(2,1)}, bf16[4,256,1792]{2,1,0:T(8,128)(2,1)}, bf16[2,1792,128]{2,1,0:T(8,128)(2,1)}, bf16[2,1792,128]{2,1,0:T(...) custom-call(bf16[256,1792]{1,0:T(8,128)(2,1)} %refs_0_.1, bf16[256,1792]{1,0:T(8,128)(2,1)} %refs_1_.1, ...), custom_call_target="tpu_custom_call" | custom-call | tf_op jit(solution)/shard_map/pallas_call | solution.py:126
  117.3 1.4 fusion.65
  118.7 2.8 %fusion.28 = bf16[128,1024]{1,0:T(8,128)(2,1)S(1)} fusion(bf16[128,1792]{1,0:T(8,128)(2,1)S(1)} %bitcast.119, bf16[1,1792,1024]{2,1,0:T(8,128)(2,1)} %param.14), kind=kOutput, calls=%fused_computation.44 | convolution fusion | flops 469893120 | bytes 4390912 | tf_op jit(solution)/shard_map/dot_general | solution.py:261
  122.2 1.3 fusion.34
  123.8 1.8 copy-done.8
  129.0 1.1 convolution_convert_fusion.6
  130.4 32.4 %shard_map.154 = (bf16[3,2,512,256]{3,2,1,0:T(8,128)(2,1)S(1)}, bf16[3,2,64,1024]{3,2,1,0:T(8,128)(2,1)S(1)}) custom-call(bf16[3,2,512,256]{3,2,1,0:T(8,128)(2,1)S(1)} %pad_maximum_fusion.refs_0_, bf16[3,2,64,1024]{3,2,1,0:T(8,128)(2,1)S(1)} %pad_maximum_fusion.6.refs_1_), custom_call_target="tpu_custom_call" | custom-call | tf_op jit(solution)/shard_map/pallas_call | solution.py:243
  162.8 1.3 fusion.2
  164.8 2.1 fusion.19
  167.0 2.1 convolution_convert_fusion
  169.0 1.2 fusion.25
  170.2 1.2 fusion.26
  172.4 1.2 fusion.23
  173.6 1.2 fusion.24
  175.7 1.1 fusion.39
  176.9 3.0 %add_convert_fusion = bf16[1024,1792]{1,0:T(8,128)(2,1)} fusion(f32[1024,1792]{1,0:T(8,128)S(1)} %fusion.39, bf16[1024,256]{1,0:T(8,128)(2,1)S(1)} %bitcast.129, bf16[1792,128]{1,0:T(8,128)(2,1)S(1)} %get-tuple-element.41, bf16[1792,128]{1,0:T(8,128)(2,1)S(1)} %get-tuple-element.40), kind=kOutput, calls=%fused_computation.4 | convolution fusion | flops 945029120 | bytes 12451840 | tf_op jit(solution)/shard_map/dot_general | solution.py:30
  179.9 80.1 %shard_map.155 = (bf16[4,256,1792]{2,1,0:T(8,128)(2,1)}, bf16[2,1792,128]{2,1,0:T(8,128)(2,1)}, bf16[2,1792,128]{2,1,0:T(8,128)(2,1)}, bf16[2,128,1792]{2,1,0:T(8,128)(2,1)}, bf16[8,16,1792]{2,1,0:T(8,128)(2,1)}) custom-call(bf16[4,256,1792]{2,1,0:T(8,128)(2,1)} %bitcast.118, bf16[2,1792,128]{2,1,0:T(8,128)(2,1)} %pad_maximum_fusion.4.refs_1_, ...), custom_call_target="tpu_custom_call" | custom-call | tf_op jit(solution)/shard_map/pallas_call | solution.py:172
  260.0 2.8 %convert_reduce_fusion = f32[256,1792]{1,0:T(8,128)S(1)} fusion(bf16[4,256,1792]{2,1,0:T(8,128)(2,1)} %get-tuple-element.28), kind=kLoop, calls=%fused_computation.3 | loop fusion | flops 3211264 | bytes 5505024 | tf_op jit(solution)/shard_map/reduce_sum | solution.py:342
  262.8 1.4 fusion.14
  267.6 3.2 %fusion.10 = bf16[1,1792,1024]{2,1,0:T(8,128)(2,1)} fusion(bf16[128,1792]{1,0:T(8,128)(2,1)S(1)} %bitcast.121, bf16[128,1024]{1,0:T(8,128)(2,1)S(1)} %bitcast.139), kind=kOutput, calls=%fused_computation.15 | convolution fusion | flops 473432064 | bytes 4390912 | tf_op jit(solution)/shard_map/dot_general | solution.py:24
  270.8 3.0 %fusion.11 = bf16[1,1792,1024]{2,1,0:T(8,128)(2,1)} fusion(bf16[128,1792]{1,0:T(8,128)(2,1)S(1)} %bitcast.122, bf16[128,1024]{1,0:T(8,128)(2,1)S(1)} %bitcast.134), kind=kOutput, calls=%fused_computation.16 | convolution fusion | flops 473432064 | bytes 4390912 | tf_op jit(solution)/shard_map/dot_general | solution.py:24
  273.8 3.0 %fusion.12 = bf16[1,1024,1792]{2,1,0:T(8,128)(2,1)} fusion(bf16[128,1024]{1,0:T(8,128)(2,1)S(1)} %bitcast.146, bf16[128,1792]{1,0:T(8,128)(2,1)S(1)} %bitcast.131), kind=kOutput, calls=%fused_computation.17 | convolution fusion | flops 473432064 | bytes 4390912 | tf_op jit(solution)/shard_map/dot_general | solution.py:24
  (50 shorter events, 14.2 us)
Async XLA Ops:
  117.3 4.2 %copy-start = (bf16[1,1792,1024]{2,1,0:T(8,128)(2,1)S(1)}, bf16[1,1792,1024]{2,1,0:T(8,128)(2,1)}, u32[]{:S(2)}) copy-start(bf16[1,1792,1024]{2,1,0:T(8,128)(2,1)} %param.15) | copy-start | bytes 11010052
  118.7 3.5 %copy-start.2 = (bf16[1,1024,1792]{2,1,0:T(8,128)(2,1)S(1)}, bf16[1,1024,1792]{2,1,0:T(8,128)(2,1)}, u32[]{:S(2)}) copy-start(bf16[1,1024,1792]{2,1,0:T(8,128)(2,1)} %param.16) | copy-start | bytes 11010052
  122.2 1.5 copy-start.3
  122.2 1.5 copy-start.4
  123.6 2.1 copy-start.8
  126.7 2.0 copy-start.9
  126.8 2.3 copy-start.10
  162.7 2.0 copy-start.1
  260.0 2.8 %copy-start.11 = (bf16[8,16,1792]{2,1,0:T(8,128)(2,1)S(1)}, bf16[8,16,1792]{2,1,0:T(8,128)(2,1)}, u32[]{:S(2)}) copy-start(bf16[8,16,1792]{2,1,0:T(8,128)(2,1)} %get-tuple-element.29) | copy-start | bytes 1376260
  262.8 1.4 copy-start.7
  262.8 2.5 copy-start.6
  264.2 2.3 copy-start.5

commit v3 on v2

--- a/solution.py
+++ b/solution.py
@@ -10,6 +10,7 @@
 CAP = 12
 SLOT = 16
 NEAR = 4
+CHUNKS = 4
 MESH = pl.DeviceIdType.MESH
 ANY = pl.BlockSpec(memory_space=pl.ANY)
 VMEM = pl.BlockSpec(memory_space=pltpu.VMEM)
@@ -82,19 +83,22 @@
     me, near, far, across, beside, corner, distant, every = expert_peers(n_exp)
     greet(every)
     pairs = ((tokens, all_tokens), (grads, all_grads))
+    rows = tokens.shape[0] // CHUNKS
     copies, relays = [], []
     for k, (src, dst) in enumerate(pairs):
-        relays.append(remote(src, dst.at[near], near_sems, 3 * k, across))
-        copies.append(remote(src, dst.at[near], near_sems, 3 * k + 1, beside))
-        relays[-1].start()
-        copies[-1].start()
+        for c in range(CHUNKS):
+            at, sem = pl.ds(c * rows, rows), 3 * (k * CHUNKS + c)
+            relays.append(remote(src.at[at], dst.at[near, at], near_sems, sem, across))
+            copies.append(remote(src.at[at], dst.at[near, at], near_sems, sem + 1, beside))
+            relays[-1].start()
+            copies[-1].start()
+        for p, peer in enumerate(distant):
+            for w in ((0, 1), (2,))[k]:
+                copies.append(remote(weights[w], all_weights[w].at[far], far_sems, 3 * p + w, peer))
+                copies[-1].start()
     for k, peer in enumerate(every):
         copies.append(remote(sends.at[peer[1]], recv.at[me], route_sems, k, peer))
         copies[-1].start()
-    for k, peer in enumerate(distant):
-        for w in range(3):
-            copies.append(remote(weights[w], all_weights[w].at[far], far_sems, 3 * k + w, peer))
-            copies[-1].start()
     own = [
         pltpu.make_async_copy(src, dst, own_sem.at[k])
         for k, (src, dst) in enumerate(
@@ -107,9 +111,11 @@
         copy.start()
     other = lax.rem(near + 2, NEAR)
     for k, (_, dst) in enumerate(pairs):
-        relays[k].wait_recv()
-        copies.append(remote(dst.at[other], dst.at[other], near_sems, 3 * k + 2, beside))
-        copies[-1].start()
+        for c in range(CHUNKS):
+            block, sem = dst.at[other, pl.ds(c * rows, rows)], 3 * (k * CHUNKS + c)
+            relays[k * CHUNKS + c].wait_recv()
+            copies.append(remote(block, block, near_sems, sem + 2, beside))
+            copies[-1].start()
     for copy in relays:
         copy.wait_send()
     for copy in own:
@@ -122,7 +128,7 @@
     n_far = n_exp // NEAR
     shapes = [(NEAR,) + a.shape for a in args[:2]] + [(n_far,) + a.shape for a in args[2:5]]
     shapes.append(args[5].shape)
-    counts = (6, 6, 3 * (n_far - 1), 3 * (n_far - 1), n_exp - 1, n_exp - 1, 6)
+    counts = (6 * CHUNKS, 6 * CHUNKS, 3 * (n_far - 1), 3 * (n_far - 1), n_exp - 1, n_exp - 1, 6)
     return pl.pallas_call(
         functools.partial(gather_kernel, n_exp),
         out_shape=[jax.ShapeDtypeStruct(shape, jnp.bfloat16) for shape in shapes],
@@ -130,52 +136,6 @@
         out_specs=[ANY] * 6,
         scratch_shapes=[pltpu.SemaphoreType.DMA((count,)) for count in counts],
         compiler_params=pltpu.CompilerParams(collective_id=1, has_side_effects=True),
-    )(*args)
-
-
-def scatter_kernel(n_exp, *refs):
-    back, *parts = refs[:4]
-    sends = refs[4]
-    got_back, *got_parts = refs[5:9]
-    recv = refs[9]
-    near_sems, far_sems, route_sems = refs[10:12], refs[12:14], refs[14:16]
-    own_sem = refs[16]
-    me, near, far, across, beside, corner, distant, every = expert_peers(n_exp)
-    greet(every)
-    copies = []
-    for k, peer in enumerate(distant):
-        for w in range(3):
-            copies.append(
-                remote(parts[w].at[peer[1] // NEAR], got_parts[w].at[far], far_sems, 3 * k + w, peer)
-            )
-    for k, peer in enumerate((corner, across, beside)):
-        copies.append(remote(back.at[lax.rem(peer[1], NEAR)], got_back.at[near], near_sems, k, peer))
-    for k, peer in enumerate(every):
-        copies.append(remote(sends.at[peer[1]], recv.at[me], route_sems, k, peer))
-    own = [
-        pltpu.make_async_copy(src, dst, own_sem.at[k])
-        for k, (src, dst) in enumerate(
-            [(back.at[near], got_back.at[near])]
-            + [(parts[w].at[far], got_parts[w].at[far]) for w in range(3)]
-            + [(sends.at[me], recv.at[me])]
-        )
-    ]
-    for copy in copies + own:
-        copy.start()
-    for copy in own + copies:
-        copy.wait()
-
-
-def scatter_call(n_exp, *args):
-    n_far = n_exp // NEAR
-    counts = (3, 3, 3 * (n_far - 1), 3 * (n_far - 1), n_exp - 1, n_exp - 1, 5)
-    return pl.pallas_call(
-        functools.partial(scatter_kernel, n_exp),
-        out_shape=[jax.ShapeDtypeStruct(a.shape, jnp.bfloat16) for a in args],
-        in_specs=[ANY] * 5,
-        out_specs=[ANY] * 5,
-        scratch_shapes=[pltpu.SemaphoreType.DMA((count,)) for count in counts],
-        compiler_params=pltpu.CompilerParams(collective_id=2, has_side_effects=True),
     )(*args)
 
 
@@ -315,41 +275,70 @@
     act, grad_gate_pre, grad_up_pre = (
         shared_acts[w].reshape(-1, n_far * width_sh) for w in range(3)
     )
-    back = contract_cols(grad_gate_pre, far_gate) + contract_cols(grad_up_pre, far_up)
-
-    def own_columns(grad_pre):
-        return jnp.stack(
-            [
-                contract_rows(all_in, grad_pre[:, k * width_sh : (k + 1) * width_sh])
-                for k in range(n_far)
-            ]
-        ).astype(jnp.bfloat16)
-
     routed_act, routed_gate, routed_up = (
         routed_acts[w].reshape(n_exp * capacity, -1) for w in range(3)
     )
+    me = lax.axis_index("expert")
+    far, high, low = me // NEAR, me % NEAR // 2, me % 2
+
+    def columns(value, index):
+        return lax.dynamic_slice_in_dim(value, index * width_sh, width_sh, axis=1)
+
+    def own_parts(index):
+        return (
+            contract_rows(all_in, columns(grad_gate_pre, index)),
+            contract_rows(all_in, columns(grad_up_pre, index)),
+            contract_rows(columns(act, index), all_grad),
+        )
+
+    def send(value, target):
+        return lax.ppermute(value, "expert", [(e, target(e)) for e in range(n_exp)])
+
+    got_parts = [
+        [
+            send(part.astype(jnp.bfloat16), lambda e: (e + k * NEAR) % n_exp)
+            for part in own_parts(lax.rem(far + k, n_far))
+        ]
+        for k in range(1, n_far)
+    ]
+
+    def back_of(index):
+        def half(value):
+            blocks = value.reshape(2, 2, -1, value.shape[1])
+            return lax.dynamic_index_in_dim(blocks, index, axis=1, keepdims=False)
+
+        gate_half, up_half = half(grad_gate_pre), half(grad_up_pre)
+        rows = gate_half.shape[0] * gate_half.shape[1]
+        back = contract_cols(gate_half.reshape(rows, -1), far_gate) + contract_cols(
+            up_half.reshape(rows, -1), far_up
+        )
+        return back.reshape(2, -1, width_dev)
+
+    got_beside = send(back_of(1 - low).astype(jnp.bfloat16), lambda e: e + 1 - e % 2 * 2)
     route_back = contract_cols(routed_gate, w_gate[0]) + contract_cols(routed_up, w_up[0])
-    got_back, got_gate, got_up, got_down, back_rows = scatter_call(
-        n_exp,
-        back.astype(jnp.bfloat16).reshape(NEAR, -1, width_dev),
-        own_columns(grad_gate_pre),
-        own_columns(grad_up_pre),
-        contract_rows(act, all_grad).astype(jnp.bfloat16).reshape(n_far, width_sh, width_dev),
+    back_rows = lax.all_to_all(
         route_back.astype(jnp.bfloat16).reshape(n_exp, capacity, width_dev),
-    )
-
-    def total(parts):
-        return jnp.sum(parts.astype(jnp.float32), axis=0)
-
+        "expert",
+        split_axis=0,
+        concat_axis=0,
+        tiled=True,
+    )
+    pair_back = back_of(low) + got_beside.astype(jnp.float32)
+    passed = lax.dynamic_index_in_dim(pair_back, 1 - high, axis=0, keepdims=False)
+    kept = lax.dynamic_index_in_dim(pair_back, high, axis=0, keepdims=False)
+    got_across = send(passed.astype(jnp.bfloat16), lambda e: e + 2 - e // 2 % 2 * 4)
     routed = jnp.einsum("tec,ecd->td", place_bf, back_rows, preferred_element_type=jnp.float32)
+    totals = own_parts(far)
+    for parts in got_parts:
+        totals = [total + part.astype(jnp.float32) for total, part in zip(totals, parts)]
     return (
-        (total(got_back) + routed).astype(jnp.bfloat16),
+        (kept + got_across.astype(jnp.float32) + routed).astype(jnp.bfloat16),
         (contract_rows(rows_in, routed_gate) * grad_scale).astype(jnp.bfloat16)[None],
         (contract_rows(rows_in, routed_up) * grad_scale).astype(jnp.bfloat16)[None],
         (contract_rows(routed_act, rows_grad) * grad_scale).astype(jnp.bfloat16)[None],
-        total(got_gate) * grad_scale,
-        total(got_up) * grad_scale,
-        total(got_down) * grad_scale,
+        totals[0] * grad_scale,
+        totals[1] * grad_scale,
+        totals[2] * grad_scale,
     )
 
 

time: 277 us -> 259 us (0.935)
  Pallas kernels: 223 us -> 141 us
  waiting for transfers between devices: 0 us -> 38.7 us
  matrix products: 36.1 us -> 51.2 us
  starting transfers between devices: 0 us -> 9.36 us
  other arithmetic: 10.7 us -> 5.76 us
  local copies, waits for them, and re-layouts: 6.5 us -> 10.9 us
    pallas_call x1 -> x0, Pallas kernels: 80.1 us -> none  [scatter_call(): pl.pallas_call(functools.partial(scatter_kernel, n_exp), out_shape=[jax.S...]
    ppermute x0 -> x5, waiting for transfers between devices: none -> 36.8 us  [send(): return lax.ppermute(value, 'expert', [(e, target(e)) for e in range(n_exp)])]
    dot_general x8 -> x9, matrix products: 15.9 us -> 26.7 us  [contract_rows(): lax.dot_general(left, right, (((0,), (0,)), ((), ())), preferred_element_...]
    ppermute x0 -> x5, starting transfers between devices: none -> 4.69 us  [send(): return lax.ppermute(value, 'expert', [(e, target(e)) for e in range(n_exp)])]
    all_to_all x0 -> x1, starting transfers between devices: none -> 4.67 us  [shards(): lax.all_to_all(route_back.astype(jnp.bfloat16).reshape(n_exp, capacity, w...]
    dot_general x6 -> x8, matrix products: 10 us -> 14 us  [contract_cols(): lax.dot_general(left, right, (((1,), (1,)), ((), ())), preferred_element_...]
    reduce_sum x4 -> x0, other arithmetic: 3.2 us -> none  [total(): return jnp.sum(parts.astype(jnp.float32), axis=0)]
    mul x3 -> x0, other arithmetic: 2.95 us -> none  [the longest x1 0.98 us: shards(): total(got_down) * grad_scale]
  transfers between devices with their start and end apart: 0 -> 6, of which waited for: 0 -> 5; matrix products, arithmetic and copies ran while one was open for 0% -> 16% of each run, Pallas kernels for 0% -> 0%
where the time goes in v3:
time: 259 us; the launch traced here: 258 us
  Pallas kernels  141 us (54%)
  matrix products  51.2 us (20%)
  waiting for transfers between devices  38.7 us (15%)
  local copies, waits for them, and re-layouts  10.9 us (4%)
  starting transfers between devices  9.36 us (4%)
  other arithmetic  5.76 us (2%)
    pallas_call x1, Pallas kernels, gather_call(): pl.pallas_call(functools.partial(gather_kernel, n_exp), out_shape=[jax.Sh...  109 us
    ppermute x5, waiting for transfers between devices, send(): return lax.ppermute(value, 'expert', [(e, target(e)) for e in range(n_exp)])  36.8 us
    pallas_call x1, Pallas kernels, hidden_call(): pl.pallas_call(functools.partial(hidden_kernel, n_dp), out_shape=[jax.Sha...  32.4 us
    dot_general x9, matrix products, contract_rows(): lax.dot_general(left, right, (((0,), (0,)), ((), ())), preferred_element_...  26.7 us
    dot_general x8, matrix products, contract_cols(): lax.dot_general(left, right, (((1,), (1,)), ((), ())), preferred_element_...  14 us
  transfers between devices with their start and end apart: 6, of which 5 were waited for; matrix products, arithmetic and copies ran while one was open for 16% of the time, Pallas kernels for 0%

profile of v3, /device:TPU:0, one launch (start us, length us, event | category | flops | bytes accessed | tf_op | source)
XLA Modules:
  0.0 257.9 jit_solution(8721896584740992687)
XLA Ops:
  7.2 108.7 %shard_map.153 = (bf16[4,256,1792]{2,1,0:T(8,128)(2,1)}, bf16[4,256,1792]{2,1,0:T(8,128)(2,1)}, bf16[2,1792,128]{2,1,0:T(8,128)(2,1)}, bf16[2,1792,128]{2,1,0:T(...) custom-call(bf16[256,1792]{1,0:T(8,128)(2,1)} %refs_0_.1, bf16[256,1792]{1,0:T(8,128)(2,1)} %refs_1_.1, ...), custom_call_target="tpu_custom_call" | custom-call | tf_op jit(solution)/shard_map/pallas_call | solution.py:132
  117.3 2.8 %fusion.24 = bf16[128,1024]{1,0:T(8,128)(2,1)S(1)} fusion(bf16[128,1792]{1,0:T(8,128)(2,1)S(1)} %bitcast.132, bf16[1,1792,1024]{2,1,0:T(8,128)(2,1)} %param.14), kind=kOutput, calls=%fused_computation.38 | convolution fusion | flops 469893120 | bytes 4390912 | tf_op jit(solution)/shard_map/dot_general | solution.py:221
  129.3 32.4 %shard_map.154 = (bf16[3,2,512,256]{3,2,1,0:T(8,128)(2,1)S(1)}, bf16[3,2,64,1024]{3,2,1,0:T(8,128)(2,1)S(1)}) custom-call(bf16[3,2,512,256]{3,2,1,0:T(8,128)(2,1)S(1)} %pad_maximum_fusion.refs_0_, bf16[3,2,64,1024]{3,2,1,0:T(8,128)(2,1)S(1)} %pad_maximum_fusion.4.refs_1_), custom_call_target="tpu_custom_call" | custom-call | tf_op jit(solution)/shard_map/pallas_call | solution.py:203
  162.8 3.7 %convolution_convert_fusion = bf16[128,1792]{1,0:T(8,128)(2,1)} fusion(bf16[1024,1792]{1,0:T(8,128)(2,1)} %bitcast.129, bf16[1024,256]{1,0:T(8,128)(2,1)} %bitcast.143, s32[]{:T(128)S(6)} %select_n.58), kind=kOutput, calls=%fused_computation.22 | convolution fusion | flops 469991424 | bytes 4390916 | tf_op jit(solution)/shard_map/dot_general | solution.py:25
  167.1 2.0 convolution_convert_fusion.1
  169.1 2.4 collective-permute-start.3
  171.4 2.0 convolution_convert_fusion.2
  177.5 2.0 add_convert_fusion
  182.2 2.1 fusion.17
  184.3 4.7 %all-to-all-start = ((bf16[8,16,1792]{2,1,0:T(8,128)(2,1)}), bf16[8,16,1792]{2,1,0:T(8,128)(2,1)}, u32[]{:S(2)}, u32[]{:S(2)}) async-start(bf16[8,16,1792]{2,1,0:T(8,128)(2,1)} %bitcast.43), calls=%async_computation | async-start | bytes 917504 | tf_op jit(solution)/shard_map/all_to_all | solution.py:319
  189.0 3.9 %fusion.10 = bf16[1,1792,1024]{2,1,0:T(8,128)(2,1)} fusion(bf16[128,1792]{1,0:T(8,128)(2,1)S(1)} %bitcast.134, bf16[128,1024]{1,0:T(8,128)(2,1)} %bitcast.157), kind=kOutput, calls=%fused_computation.16 | convolution fusion | flops 473432064 | bytes 4390912 | tf_op jit(solution)/shard_map/dot_general | solution.py:25
  192.9 3.0 %fusion.11 = bf16[1,1792,1024]{2,1,0:T(8,128)(2,1)} fusion(bf16[128,1792]{1,0:T(8,128)(2,1)S(1)} %bitcast.135, bf16[128,1024]{1,0:T(8,128)(2,1)S(1)} %bitcast.154), kind=kOutput, calls=%fused_computation.17 | convolution fusion | flops 473432064 | bytes 4390912 | tf_op jit(solution)/shard_map/dot_general | solution.py:25
  195.9 2.6 %fusion.37 = f32[512,1792]{1,0:T(8,128)} fusion(bf16[512,256]{1,0:T(8,128)(2,1)S(1)} %bitcast.147, bf16[1792,128]{1,0:T(8,128)(2,1)S(1)} %get-tuple-element.41, bf16[1792,128]{1,0:T(8,128)(2,1)S(1)} %get-tuple-element.42), kind=kOutput, calls=%fused_computation.56 | convolution fusion | flops 471597056 | bytes 4849664 | tf_op jit(solution)/shard_map/dot_general | solution.py:31
  198.5 3.0 %fusion.12 = bf16[1,1024,1792]{2,1,0:T(8,128)(2,1)} fusion(bf16[128,1024]{1,0:T(8,128)(2,1)S(1)} %bitcast.162, bf16[128,1792]{1,0:T(8,128)(2,1)S(1)} %bitcast.146), kind=kOutput, calls=%fused_computation.18 | convolution fusion | flops 473432064 | bytes 4390912 | tf_op jit(solution)/shard_map/dot_general | solution.py:25
  201.5 2.9 %convolution_add_fusion = f32[512,1792]{1,0:T(8,128)S(1)} fusion(f32[512,1792]{1,0:T(8,128)} %fusion.37, bf16[512,256]{1,0:T(8,128)(2,1)S(1)} %bitcast.149, bf16[1792,128]{1,0:T(8,128)(2,1)S(1)} %get-tuple-element.31, bf16[1792,128]{1,0:T(8,128)(2,1)S(1)} %get-tuple-element.30), kind=kOutput, calls=%fused_computation.15 | convolution fusion | flops 472514560 | bytes 8519680 | tf_op jit(solution)/shard_map/dot_general | solution.py:31
  204.4 10.6 %collective-permute-done.4 = bf16[128,1792]{1,0:T(8,128)(2,1)} collective-permute-done((bf16[128,1792]{1,0:T(8,128)(2,1)}, bf16[128,1792]{1,0:T(8,128)(2,1)}, u32[]{:S(2)}, u32[]{:S(2)}) %collective-permute-start.4) | collective-permute-done | bytes 458784 | tf_op jit(solution)/shard_map/ppermute | solution.py:295
  215.0 2.6 %add_multiply_fusion = f32[128,1792]{1,0:T(8,128)} fusion(bf16[128,1792]{1,0:T(8,128)(2,1)} %collective-permute-done.4, bf16[1024,1792]{1,0:T(8,128)(2,1)S(1)} %bitcast.131, bf16[1024,256]{1,0:T(8,128)(2,1)S(1)} %bitcast.144, s32[]{:T(128)S(6)} %select_n.57), kind=kOutput, calls=%fused_computation.47 | convolution fusion | flops 470450176 | bytes 5308420 | tf_op jit(solution)/shard_map/dot_general | solution.py:25
  217.6 6.7 %collective-permute-done = bf16[2,256,1792]{2,1,0:T(8,128)(2,1)} collective-permute-done((bf16[2,256,1792]{2,1,0:T(8,128)(2,1)}, bf16[2,256,1792]{2,1,0:T(8,128)(2,1)}, u32[]{:S(2)}, u32[]{:S(2)}) %collective-permute-start) | collective-permute-done | bytes 1835040 | tf_op jit(solution)/shard_map/ppermute | solution.py:295
  224.3 2.0 convert_add_fusion
  227.1 3.5 %add_multiply_fusion.1 = f32[1792,128]{1,0:T(8,128)} fusion(bf16[1792,128]{1,0:T(8,128)(2,1)} %collective-permute-done.3, bf16[1024,1792]{1,0:T(8,128)(2,1)S(1)} %bitcast.126, bf16[1024,256]{1,0:T(8,128)(2,1)S(1)} %bitcast.142, s32[]{:T(128)S(6)} %select_n.57), kind=kOutput, calls=%fused_computation.48 | convolution fusion | flops 470450176 | bytes 5308420 | tf_op jit(solution)/shard_map/dot_general | solution.py:25
  230.6 4.2 %collective-permute-done.2 = bf16[1792,128]{1,0:T(8,128)(2,1)} collective-permute-done((bf16[1792,128]{1,0:T(8,128)(2,1)}, bf16[1792,128]{1,0:T(8,128)(2,1)}, u32[]{:S(2)}, u32[]{:S(2)}) %collective-permute-start.2) | collective-permute-done | bytes 458784 | tf_op jit(solution)/shard_map/ppermute | solution.py:295
  234.7 3.1 %add_multiply_fusion.2 = f32[1792,128]{1,0:T(8,128)} fusion(bf16[1792,128]{1,0:T(8,128)(2,1)} %collective-permute-done.2, bf16[1024,1792]{1,0:T(8,128)(2,1)S(1)} %bitcast.127, bf16[1024,256]{1,0:T(8,128)(2,1)S(1)} %bitcast.139, s32[]{:T(128)S(6)} %select_n.57), kind=kOutput, calls=%fused_computation.49 | convolution fusion | flops 470450176 | bytes 5308420 | tf_op jit(solution)/shard_map/dot_general | solution.py:25
  237.8 1.9 all-to-all-done
  241.3 15.3 %collective-permute-done.1 = bf16[256,1792]{1,0:T(8,128)(2,1)S(1)} collective-permute-done((bf16[256,1792]{1,0:T(8,128)(2,1)S(1)}, bf16[256,1792]{1,0:T(8,128)(2,1)S(1)}, u32[]{:S(2)}, u32[]{:S(2)}) %collective-permute-start.1) | collective-permute-done | bytes 917536 | tf_op jit(solution)/shard_map/ppermute | solution.py:295
  (88 shorter events, 29.1 us)
Async XLA Ops:
  115.9 4.2 %copy-start.3 = (bf16[1,1792,1024]{2,1,0:T(8,128)(2,1)S(1)}, bf16[1,1792,1024]{2,1,0:T(8,128)(2,1)}, u32[]{:S(2)}) copy-start(bf16[1,1792,1024]{2,1,0:T(8,128)(2,1)} %param.15) | copy-start | bytes 11010052
  117.3 3.6 %copy-start.22 = (bf16[2,1792,128]{2,1,0:T(8,128)(2,1)S(1)}, bf16[2,1792,128]{2,1,0:T(8,128)(2,1)}, u32[]{:S(2)}) copy-start(bf16[2,1792,128]{2,1,0:T(8,128)(2,1)} %get-tuple-element.16) | copy-start | bytes 2752516
  117.3 3.6 %copy-start.23 = (bf16[2,1792,128]{2,1,0:T(8,128)(2,1)S(1)}, bf16[2,1792,128]{2,1,0:T(8,128)(2,1)}, u32[]{:S(2)}) copy-start(bf16[2,1792,128]{2,1,0:T(8,128)(2,1)} %get-tuple-element.17) | copy-start | bytes 2752516
  162.8 4.3 %copy-start.1 = (bf16[4,256,1792]{2,1,0:T(8,128)(2,1)S(1)}, bf16[4,256,1792]{2,1,0:T(8,128)(2,1)}, u32[]{:S(2)}) copy-start(bf16[4,256,1792]{2,1,0:T(8,128)(2,1)} %get-tuple-element.15) | copy-start | bytes 11010052
  162.8 4.3 %copy-start.13 = (bf16[1,2,512,256]{3,2,1,0:T(8,128)(2,1)S(1)}, bf16[1,2,512,256]{3,2,1,0:T(8,128)(2,1)}, u32[]{:S(2)}) copy-start(bf16[1,2,512,256]{3,2,1,0:T(8,128)(2,1)} %get-tuple-element.24) | copy-start | bytes 1572868
  166.5 4.9 %copy-start.11 = (bf16[1,2,512,256]{3,2,1,0:T(8,128)(2,1)S(1)}, bf16[1,2,512,256]{3,2,1,0:T(8,128)(2,1)}, u32[]{:S(2)}) copy-start(bf16[1,2,512,256]{3,2,1,0:T(8,128)(2,1)} %get-tuple-element.25) | copy-start | bytes 1572868
  166.5 48.5 %collective-permute-start.4 = (bf16[128,1792]{1,0:T(8,128)(2,1)}, bf16[128,1792]{1,0:T(8,128)(2,1)}, u32[]{:S(2)}, u32[]{:S(2)}) collective-permute-start(bf16[128,1792]{1,0:T(8,128)(2,1)} %convolution_convert_fusion), channel_id=1, source_target_pairs={{0,4},{1,5},{2,6},{3,7},{4,0},{5,1},{6,2},{7,3},{8,12},{9,13},{10,... | collective-permute-start | bytes 1376264 | tf_op jit(solution)/shard_map/ppermute | solution.py:295
  169.1 58.0 %collective-permute-start.3 = (bf16[1792,128]{1,0:T(8,128)(2,1)}, bf16[1792,128]{1,0:T(8,128)(2,1)}, u32[]{:S(2)}, u32[]{:S(2)}) collective-permute-start(bf16[1792,128]{1,0:T(8,128)(2,1)} %convolution_convert_fusion.1), channel_id=1, source_target_pairs={{0,4},{1,5},{2,6},{3,7},{4,0},{5,1},{6,2},{7,3},{8,12},{9,13},{10,... | collective-permute-start | bytes 1376264 | tf_op jit(solution)/shard_map/ppermute | solution.py:295
  173.4 61.3 %collective-permute-start.2 = (bf16[1792,128]{1,0:T(8,128)(2,1)}, bf16[1792,128]{1,0:T(8,128)(2,1)}, u32[]{:S(2)}, u32[]{:S(2)}) collective-permute-start(bf16[1792,128]{1,0:T(8,128)(2,1)} %convolution_convert_fusion.2), channel_id=1, source_target_pairs={{0,4},{1,5},{2,6},{3,7},{4,0},{5,1},{6,2},{7,3},{8,12},{9,13},{10,... | collective-permute-start | bytes 1376264 | tf_op jit(solution)/shard_map/ppermute | solution.py:295
  177.5 3.3 %copy-start.4 = (bf16[1,1792,1024]{2,1,0:T(8,128)(2,1)S(1)}, bf16[1,1792,1024]{2,1,0:T(8,128)(2,1)}, u32[]{:S(2)}) copy-start(bf16[1,1792,1024]{2,1,0:T(8,128)(2,1)} %param.15) | copy-start | bytes 11010052
  179.5 44.8 %collective-permute-start = (bf16[2,256,1792]{2,1,0:T(8,128)(2,1)}, bf16[2,256,1792]{2,1,0:T(8,128)(2,1)}, u32[]{:S(2)}, u32[]{:S(2)}) collective-permute-start(bf16[2,256,1792]{2,1,0:T(8,128)(2,1)} %bitcast.38), channel_id=1, source_target_pairs={{0,1},{1,0},{2,3},{3,2},{4,5},{5,4},{6,7},{7,6},{8,9},{9,8},{10,11... | collective-permute-start | bytes 5505032 | tf_op jit(solution)/shard_map/ppermute | solution.py:295
  180.8 3.5 %copy-start.21 = (bf16[1,2,64,1024]{3,2,1,0:T(8,128)(2,1)}, bf16[1,2,64,1024]{3,2,1,0:T(8,128)(2,1)S(1)}, u32[]{:S(2)}) copy-start(bf16[1,2,64,1024]{3,2,1,0:T(8,128)(2,1)S(1)} %get-tuple-element.34) | copy-start | bytes 786436
  184.3 8.6 %copy-start.20 = (bf16[1,2,64,1024]{3,2,1,0:T(8,128)(2,1)S(1)}, bf16[1,2,64,1024]{3,2,1,0:T(8,128)(2,1)}, u32[]{:S(2)}) copy-start(bf16[1,2,64,1024]{3,2,1,0:T(8,128)(2,1)} %copy-done.19) | copy-start | bytes 786436
  184.3 55.4 %all-to-all-start = ((bf16[8,16,1792]{2,1,0:T(8,128)(2,1)}), bf16[8,16,1792]{2,1,0:T(8,128)(2,1)}, u32[]{:S(2)}, u32[]{:S(2)}) async-start(bf16[8,16,1792]{2,1,0:T(8,128)(2,1)} %bitcast.43), calls=%async_computation | async-start | bytes 917504 | tf_op jit(solution)/shard_map/all_to_all | solution.py:319
  192.9 3.0 %copy-start.17 = (bf16[2,1,256,256]{3,2,1,0:T(8,128)(2,1)S(1)}, bf16[2,1,256,256]{3,2,1,0:T(8,128)(2,1)}, u32[]{:S(2)}) copy-start(bf16[2,1,256,256]{3,2,1,0:T(8,128)(2,1)} %get-tuple-element.38) | copy-start | bytes 786436
  198.5 3.0 %copy-start.18 = (bf16[2,1,256,256]{3,2,1,0:T(8,128)(2,1)S(1)}, bf16[2,1,256,256]{3,2,1,0:T(8,128)(2,1)}, u32[]{:S(2)}) copy-start(bf16[2,1,256,256]{3,2,1,0:T(8,128)(2,1)} %get-tuple-element.36) | copy-start | bytes 786436
  201.5 13.5 %copy-start.7 = (bf16[4,256,1792]{2,1,0:T(8,128)(2,1)S(1)}, bf16[4,256,1792]{2,1,0:T(8,128)(2,1)}, u32[]{:S(2)}) copy-start(bf16[4,256,1792]{2,1,0:T(8,128)(2,1)} %get-tuple-element.18) | copy-start | bytes 11010052
  201.5 13.5 %copy-start.16 = (bf16[1,2,512,256]{3,2,1,0:T(8,128)(2,1)S(1)}, bf16[1,2,512,256]{3,2,1,0:T(8,128)(2,1)}, u32[]{:S(2)}) copy-start(bf16[1,2,512,256]{3,2,1,0:T(8,128)(2,1)} %get-tuple-element.23) | copy-start | bytes 1572868
  224.3 2.8 %copy-start.2 = (bf16[4,256,1792]{2,1,0:T(8,128)(2,1)S(1)}, bf16[4,256,1792]{2,1,0:T(8,128)(2,1)}, u32[]{:S(2)}) copy-start(bf16[4,256,1792]{2,1,0:T(8,128)(2,1)} %get-tuple-element.15) | copy-start | bytes 11010052
  224.3 2.8 %copy-start.15 = (bf16[1,2,512,256]{3,2,1,0:T(8,128)(2,1)S(1)}, bf16[1,2,512,256]{3,2,1,0:T(8,128)(2,1)}, u32[]{:S(2)}) copy-start(bf16[1,2,512,256]{3,2,1,0:T(8,128)(2,1)} %get-tuple-element.24) | copy-start | bytes 1572868
  226.3 4.2 %copy-start.8 = (f32[2,256,1792]{2,1,0:T(8,128)}, f32[2,256,1792]{2,1,0:T(8,128)S(1)}, u32[]{:S(2)}) copy-start(f32[2,256,1792]{2,1,0:T(8,128)S(1)} %convert_add_fusion) | copy-start | bytes 11010052
  226.5 8.3 %copy-start.12 = (bf16[1,2,512,256]{3,2,1,0:T(8,128)(2,1)S(1)}, bf16[1,2,512,256]{3,2,1,0:T(8,128)(2,1)}, u32[]{:S(2)}) copy-start(bf16[1,2,512,256]{3,2,1,0:T(8,128)(2,1)} %get-tuple-element.25) | copy-start | bytes 1572868
  226.5 30.2 %collective-permute-start.1 = (bf16[256,1792]{1,0:T(8,128)(2,1)S(1)}, bf16[256,1792]{1,0:T(8,128)(2,1)S(1)}, u32[]{:S(2)}, u32[]{:S(2)}) collective-permute-start(bf16[256,1792]{1,0:T(8,128)(2,1)S(1)} %fusion.33), channel_id=1, source_target_pairs={{0,2},{1,3},{2,0},{3,1},{4,6},{5,7},{6,4},{7,5},{8,10},{9,11},{10,... | collective-permute-start | bytes 2752520 | tf_op jit(solution)/shard_map/ppermute | solution.py:295
  239.7 17.0 %copy-start.9 = (f32[2,256,1792]{2,1,0:T(8,128)S(1)}, f32[2,256,1792]{2,1,0:T(8,128)}, u32[]{:S(2)}) copy-start(f32[2,256,1792]{2,1,0:T(8,128)} %copy-done.8) | copy-start | bytes 11010052
  (8 other events, 16.1 us)

commit v4 on v3

--- a/solution.py
+++ b/solution.py
@@ -294,6 +294,23 @@
     def send(value, target):
         return lax.ppermute(value, "expert", [(e, target(e)) for e in range(n_exp)])
 
+    def back_of(index):
+        def block(value):
+            blocks = value.reshape(NEAR, -1, value.shape[1])
+            return lax.dynamic_index_in_dim(blocks, index, axis=0, keepdims=False)
+
+        return contract_cols(block(grad_gate_pre), far_gate) + contract_cols(
+            block(grad_up_pre), far_up
+        )
+
+    def beside(e):
+        return e + 1 - e % 2 * 2
+
+    corner_back = back_of((1 - high) * 2 + 1 - low).astype(jnp.bfloat16)
+    corner_back, act, grad_gate_pre, grad_up_pre, routed_gate, routed_up = lax.optimization_barrier(
+        (corner_back, act, grad_gate_pre, grad_up_pre, routed_gate, routed_up)
+    )
+    got_corner = send(corner_back, beside)
     got_parts = [
         [
             send(part.astype(jnp.bfloat16), lambda e: (e + k * NEAR) % n_exp)
@@ -302,19 +319,7 @@
         for k in range(1, n_far)
     ]
 
-    def back_of(index):
-        def half(value):
-            blocks = value.reshape(2, 2, -1, value.shape[1])
-            return lax.dynamic_index_in_dim(blocks, index, axis=1, keepdims=False)
-
-        gate_half, up_half = half(grad_gate_pre), half(grad_up_pre)
-        rows = gate_half.shape[0] * gate_half.shape[1]
-        back = contract_cols(gate_half.reshape(rows, -1), far_gate) + contract_cols(
-            up_half.reshape(rows, -1), far_up
-        )
-        return back.reshape(2, -1, width_dev)
-
-    got_beside = send(back_of(1 - low).astype(jnp.bfloat16), lambda e: e + 1 - e % 2 * 2)
+    got_beside = send(back_of(high * 2 + 1 - low).astype(jnp.bfloat16), beside)
     route_back = contract_cols(routed_gate, w_gate[0]) + contract_cols(routed_up, w_up[0])
     back_rows = lax.all_to_all(
         route_back.astype(jnp.bfloat16).reshape(n_exp, capacity, width_dev),
@@ -323,10 +328,9 @@
         concat_axis=0,
         tiled=True,
     )
-    pair_back = back_of(low) + got_beside.astype(jnp.float32)
-    passed = lax.dynamic_index_in_dim(pair_back, 1 - high, axis=0, keepdims=False)
-    kept = lax.dynamic_index_in_dim(pair_back, high, axis=0, keepdims=False)
+    passed = back_of((1 - high) * 2 + low) + got_corner.astype(jnp.float32)
     got_across = send(passed.astype(jnp.bfloat16), lambda e: e + 2 - e // 2 % 2 * 4)
+    kept = back_of(me % NEAR) + got_beside.astype(jnp.float32)
     routed = jnp.einsum("tec,ecd->td", place_bf, back_rows, preferred_element_type=jnp.float32)
     totals = own_parts(far)
     for parts in got_parts:

time: 259 us -> 264 us (1.019)
  waiting for transfers between devices: 38.7 us -> 44.7 us
    ppermute x5 -> x6, waiting for transfers between devices: 36.8 us -> 42.4 us  [send(): return lax.ppermute(value, 'expert', [(e, target(e)) for e in range(n_exp)])]
    unnamed x52 -> x36, local copies, waits for them, and re-layouts: 3.67 us -> 5.44 us
    dot_general x8 -> x12, matrix products: 14 us -> 15.2 us  [contract_cols(): lax.dot_general(left, right, (((1,), (1,)), ((), ())), preferred_element_...]
    ppermute x5 -> x6, starting transfers between devices: 4.69 us -> 5.59 us  [send(): return lax.ppermute(value, 'expert', [(e, target(e)) for e in range(n_exp)])]
  transfers between devices with their start and end apart: 6 -> 7, of which waited for: 5 -> 5; matrix products, arithmetic and copies ran while one was open for 16% -> 13% of each run, Pallas kernels for 0% -> 0%
where the time goes in v4:
time: 264 us; the launch traced here: 263 us
  Pallas kernels  141 us (53%)
  matrix products  51.6 us (20%)
  waiting for transfers between devices  44.7 us (17%)
  local copies, waits for them, and re-layouts  9.93 us (4%)
  starting transfers between devices  9.93 us (4%)
  other arithmetic  5.07 us (2%)
    pallas_call x1, Pallas kernels, gather_call(): pl.pallas_call(functools.partial(gather_kernel, n_exp), out_shape=[jax.Sh...  109 us
    ppermute x6, waiting for transfers between devices, send(): return lax.ppermute(value, 'expert', [(e, target(e)) for e in range(n_exp)])  42.4 us
    pallas_call x1, Pallas kernels, hidden_call(): pl.pallas_call(functools.partial(hidden_kernel, n_dp), out_shape=[jax.Sha...  32.4 us
    dot_general x9, matrix products, contract_rows(): lax.dot_general(left, right, (((0,), (0,)), ((), ())), preferred_element_...  27.2 us
    dot_general x12, matrix products, contract_cols(): lax.dot_general(left, right, (((1,), (1,)), ((), ())), preferred_element_...  15.2 us
    ppermute x6, starting transfers between devices, send(): return lax.ppermute(value, 'expert', [(e, target(e)) for e in range(n_exp)])  5.59 us
    unnamed x36, local copies, waits for them, and re-layouts  5.44 us
  transfers between devices with their start and end apart: 7, of which 5 were waited for; matrix products, arithmetic and copies ran while one was open for 13% of the time, Pallas kernels for 0%

profile of v4, /device:TPU:0, one launch (start us, length us, event | category | flops | bytes accessed | tf_op | source)
XLA Modules:
  0.0 263.2 jit_solution(16959113102115447017)
XLA Ops:
  6.2 108.7 %shard_map.153 = (bf16[4,256,1792]{2,1,0:T(8,128)(2,1)}, bf16[4,256,1792]{2,1,0:T(8,128)(2,1)}, bf16[2,1792,128]{2,1,0:T(8,128)(2,1)}, bf16[2,1792,128]{2,1,0:T(...) custom-call(bf16[256,1792]{1,0:T(8,128)(2,1)} %refs_0_.1, bf16[256,1792]{1,0:T(8,128)(2,1)} %refs_1_.1, ...), custom_call_target="tpu_custom_call" | custom-call | tf_op jit(solution)/shard_map/pallas_call | solution.py:132
  116.1 2.8 %fusion.27 = bf16[128,1024]{1,0:T(8,128)(2,1)S(1)} fusion(bf16[128,1792]{1,0:T(8,128)(2,1)S(1)} %bitcast.141, bf16[1,1792,1024]{2,1,0:T(8,128)(2,1)} %param.15), kind=kOutput, calls=%fused_computation.40 | convolution fusion | flops 469893120 | bytes 4390912 | tf_op jit(solution)/shard_map/dot_general | solution.py:222
  125.0 1.9 copy-done
  129.4 32.4 %shard_map.154 = (bf16[3,2,512,256]{3,2,1,0:T(8,128)(2,1)S(1)}, bf16[3,2,64,1024]{3,2,1,0:T(8,128)(2,1)S(1)}) custom-call(bf16[3,2,512,256]{3,2,1,0:T(8,128)(2,1)S(1)} %pad_maximum_fusion.refs_0_, bf16[3,2,64,1024]{3,2,1,0:T(8,128)(2,1)S(1)} %pad_maximum_fusion.4.refs_1_), custom_call_target="tpu_custom_call" | custom-call | tf_op jit(solution)/shard_map/pallas_call | solution.py:203
  164.1 2.3 fusion.13
  166.4 4.1 %convolution_convert_fusion.1 = bf16[1792,128]{1,0:T(8,128)(2,1)} fusion(bf16[1024,1792]{1,0:T(8,128)(2,1)} %bitcast.132, bf16[1024,256]{1,0:T(8,128)(2,1)} %bitcast.153, s32[]{:T(128)S(6)} %select_n.61), kind=kOutput, calls=%fused_computation.26 | convolution fusion | flops 469991424 | bytes 4390916 | tf_op jit(solution)/shard_map/dot_general | solution.py:25
  171.2 1.9 convolution_convert_fusion.2
  173.1 2.3 collective-permute-start.3
  179.0 2.1 fusion.19
  181.1 4.3 %all-to-all-start = ((bf16[8,16,1792]{2,1,0:T(8,128)(2,1)}), bf16[8,16,1792]{2,1,0:T(8,128)(2,1)}, u32[]{:S(2)}, u32[]{:S(2)}) async-start(bf16[8,16,1792]{2,1,0:T(8,128)(2,1)} %bitcast.162), calls=%async_computation | async-start | bytes 917504 | tf_op jit(solution)/shard_map/all_to_all | solution.py:324
  187.6 2.3 fusion.14
  190.3 3.9 %fusion.10 = bf16[1,1792,1024]{2,1,0:T(8,128)(2,1)} fusion(bf16[128,1792]{1,0:T(8,128)(2,1)S(1)} %bitcast.143, bf16[128,1024]{1,0:T(8,128)(2,1)} %bitcast.168), kind=kOutput, calls=%fused_computation.13 | convolution fusion | flops 473432064 | bytes 4390912 | tf_op jit(solution)/shard_map/dot_general | solution.py:25
  194.2 3.0 %fusion.11 = bf16[1,1792,1024]{2,1,0:T(8,128)(2,1)} fusion(bf16[128,1792]{1,0:T(8,128)(2,1)S(1)} %bitcast.144, bf16[128,1024]{1,0:T(8,128)(2,1)S(1)} %bitcast.164), kind=kOutput, calls=%fused_computation.14 | convolution fusion | flops 473432064 | bytes 4390912 | tf_op jit(solution)/shard_map/dot_general | solution.py:25
  197.2 3.9 %fusion.12 = bf16[1,1024,1792]{2,1,0:T(8,128)(2,1)} fusion(bf16[128,1024]{1,0:T(8,128)(2,1)} %bitcast.174, bf16[128,1792]{1,0:T(8,128)(2,1)S(1)} %bitcast.161), kind=kOutput, calls=%fused_computation.15 | convolution fusion | flops 473432064 | bytes 4390912 | tf_op jit(solution)/shard_map/dot_general | solution.py:25
  203.1 16.0 %collective-permute-done.4 = bf16[1792,128]{1,0:T(8,128)(2,1)} collective-permute-done((bf16[1792,128]{1,0:T(8,128)(2,1)}, bf16[1792,128]{1,0:T(8,128)(2,1)}, u32[]{:S(2)}, u32[]{:S(2)}) %collective-permute-start.4) | collective-permute-done | bytes 458784 | tf_op jit(solution)/shard_map/ppermute | solution.py:295
  219.1 3.1 %add_multiply_fusion.1 = f32[1792,128]{1,0:T(8,128)} fusion(bf16[1792,128]{1,0:T(8,128)(2,1)} %collective-permute-done.4, bf16[1024,1792]{1,0:T(8,128)(2,1)S(1)} %bitcast.136, bf16[1024,256]{1,0:T(8,128)(2,1)S(1)} %bitcast.156, s32[]{:T(128)S(6)} %select_n.60), kind=kOutput, calls=%fused_computation.48 | convolution fusion | flops 470450176 | bytes 5308420 | tf_op jit(solution)/shard_map/dot_general | solution.py:25
  222.2 2.6 add_convert_fusion.1
  224.8 4.2 %collective-permute-done.3 = bf16[1792,128]{1,0:T(8,128)(2,1)} collective-permute-done((bf16[1792,128]{1,0:T(8,128)(2,1)}, bf16[1792,128]{1,0:T(8,128)(2,1)}, u32[]{:S(2)}, u32[]{:S(2)}) %collective-permute-start.3) | collective-permute-done | bytes 458784 | tf_op jit(solution)/shard_map/ppermute | solution.py:295
  229.0 3.1 %add_multiply_fusion.2 = f32[1792,128]{1,0:T(8,128)} fusion(bf16[1792,128]{1,0:T(8,128)(2,1)} %collective-permute-done.3, bf16[1024,1792]{1,0:T(8,128)(2,1)S(1)} %bitcast.137, bf16[1024,256]{1,0:T(8,128)(2,1)S(1)} %bitcast.151, s32[]{:T(128)S(6)} %select_n.60), kind=kOutput, calls=%fused_computation.49 | convolution fusion | flops 470450176 | bytes 5308420 | tf_op jit(solution)/shard_map/dot_general | solution.py:25
  232.1 6.7 %collective-permute-done.5 = bf16[128,1792]{1,0:T(8,128)(2,1)} collective-permute-done((bf16[128,1792]{1,0:T(8,128)(2,1)}, bf16[128,1792]{1,0:T(8,128)(2,1)}, u32[]{:S(2)}, u32[]{:S(2)}) %collective-permute-start.5) | collective-permute-done | bytes 458784 | tf_op jit(solution)/shard_map/ppermute | solution.py:295
  238.8 2.6 add_multiply_fusion
  241.4 2.3 all-to-all-done
  245.2 15.5 %collective-permute-done.2 = bf16[256,1792]{1,0:T(8,128)(2,1)S(1)} collective-permute-done((bf16[256,1792]{1,0:T(8,128)(2,1)}, bf16[256,1792]{1,0:T(8,128)(2,1)S(1)}, u32[]{:S(2)}, u32[]{:S(2)}) %collective-permute-start.2) | collective-permute-done | bytes 917536 | tf_op jit(solution)/shard_map/ppermute | solution.py:295
  260.7 2.5 add_convert_fusion
  (74 shorter events, 27.5 us)
Async XLA Ops:
  0.6 4.2 %copy-start.10 = (bf16[256,1792]{1,0:T(8,128)(2,1)S(1)}, bf16[256,1792]{1,0:T(8,128)(2,1)}, u32[]{:S(2)}) copy-start(bf16[256,1792]{1,0:T(8,128)(2,1)} %refs_1_.1) | copy-start | bytes 2752516
  116.1 3.1 %copy-start.4 = (bf16[1,1792,1024]{2,1,0:T(8,128)(2,1)S(1)}, bf16[1,1792,1024]{2,1,0:T(8,128)(2,1)}, u32[]{:S(2)}) copy-start(bf16[1,1792,1024]{2,1,0:T(8,128)(2,1)} %param.14) | copy-start | bytes 11010052
  116.1 3.8 %copy-start.17 = (bf16[2,128,1792]{2,1,0:T(8,128)(2,1)S(1)}, bf16[2,128,1792]{2,1,0:T(8,128)(2,1)}, u32[]{:S(2)}) copy-start(bf16[2,128,1792]{2,1,0:T(8,128)(2,1)} %get-tuple-element.25) | copy-start | bytes 2752516
  119.3 2.1 copy-start.6
  121.4 2.0 copy-start.9
  123.4 1.3 copy-start.15
  123.4 1.5 copy-start.16
  124.8 2.0 copy-start
  166.4 4.7 %copy-start.1 = (bf16[4,256,1792]{2,1,0:T(8,128)(2,1)S(1)}, bf16[4,256,1792]{2,1,0:T(8,128)(2,1)}, u32[]{:S(2)}) copy-start(bf16[4,256,1792]{2,1,0:T(8,128)(2,1)} %get-tuple-element.21) | copy-start | bytes 11010052
  170.6 4.9 %copy-start.7 = (bf16[4,256,1792]{2,1,0:T(8,128)(2,1)S(1)}, bf16[4,256,1792]{2,1,0:T(8,128)(2,1)}, u32[]{:S(2)}) copy-start(bf16[4,256,1792]{2,1,0:T(8,128)(2,1)} %get-tuple-element.24) | copy-start | bytes 11010052
  170.6 4.9 %copy-start.12 = (bf16[1,2,512,256]{3,2,1,0:T(8,128)(2,1)S(1)}, bf16[1,2,512,256]{3,2,1,0:T(8,128)(2,1)}, u32[]{:S(2)}) copy-start(bf16[1,2,512,256]{3,2,1,0:T(8,128)(2,1)} %get-tuple-element.35) | copy-start | bytes 1572868
  170.6 48.5 %collective-permute-start.4 = (bf16[1792,128]{1,0:T(8,128)(2,1)}, bf16[1792,128]{1,0:T(8,128)(2,1)}, u32[]{:S(2)}, u32[]{:S(2)}) collective-permute-start(bf16[1792,128]{1,0:T(8,128)(2,1)} %convolution_convert_fusion.1), channel_id=1, source_target_pairs={{0,4},{1,5},{2,6},{3,7},{4,0},{5,1},{6,2},{7,3},{8,12},{9,13},{10,... | collective-permute-start | bytes 1376264 | tf_op jit(solution)/shard_map/ppermute | solution.py:295
  173.1 4.4 %copy-start.3 = (bf16[1,1792,1024]{2,1,0:T(8,128)(2,1)S(1)}, bf16[1,1792,1024]{2,1,0:T(8,128)(2,1)}, u32[]{:S(2)}) copy-start(bf16[1,1792,1024]{2,1,0:T(8,128)(2,1)} %param.15) | copy-start | bytes 11010052
  173.1 55.9 %collective-permute-start.3 = (bf16[1792,128]{1,0:T(8,128)(2,1)}, bf16[1792,128]{1,0:T(8,128)(2,1)}, u32[]{:S(2)}, u32[]{:S(2)}) collective-permute-start(bf16[1792,128]{1,0:T(8,128)(2,1)} %convolution_convert_fusion.2), channel_id=1, source_target_pairs={{0,4},{1,5},{2,6},{3,7},{4,0},{5,1},{6,2},{7,3},{8,12},{9,13},{10,... | collective-permute-start | bytes 1376264 | tf_op jit(solution)/shard_map/ppermute | solution.py:295
  176.9 2.0 copy-start.5
  177.0 2.1 copy-start.14
  177.0 61.9 %collective-permute-start.5 = (bf16[128,1792]{1,0:T(8,128)(2,1)}, bf16[128,1792]{1,0:T(8,128)(2,1)}, u32[]{:S(2)}, u32[]{:S(2)}) collective-permute-start(bf16[128,1792]{1,0:T(8,128)(2,1)} %convolution_convert_fusion), channel_id=1, source_target_pairs={{0,4},{1,5},{2,6},{3,7},{4,0},{5,1},{6,2},{7,3},{8,12},{9,13},{10,... | collective-permute-start | bytes 1376264 | tf_op jit(solution)/shard_map/ppermute | solution.py:295
  181.1 62.6 %all-to-all-start = ((bf16[8,16,1792]{2,1,0:T(8,128)(2,1)}), bf16[8,16,1792]{2,1,0:T(8,128)(2,1)}, u32[]{:S(2)}, u32[]{:S(2)}) async-start(bf16[8,16,1792]{2,1,0:T(8,128)(2,1)} %bitcast.162), calls=%async_computation | async-start | bytes 917504 | tf_op jit(solution)/shard_map/all_to_all | solution.py:324
  185.5 36.8 %collective-permute-start.1 = (bf16[256,1792]{1,0:T(8,128)(2,1)}, bf16[256,1792]{1,0:T(8,128)(2,1)}, u32[]{:S(2)}, u32[]{:S(2)}) collective-permute-start(bf16[256,1792]{1,0:T(8,128)(2,1)} %fusion.13), channel_id=1, source_target_pairs={{0,1},{1,0},{2,3},{3,2},{4,5},{5,4},{6,7},{7,6},{8,9},{9,8},{10,11... | collective-permute-start | bytes 2752520 | tf_op jit(solution)/shard_map/ppermute | solution.py:295
  189.9 55.3 %collective-permute-start = (bf16[256,1792]{1,0:T(8,128)(2,1)}, bf16[256,1792]{1,0:T(8,128)(2,1)}, u32[]{:S(2)}, u32[]{:S(2)}) collective-permute-start(bf16[256,1792]{1,0:T(8,128)(2,1)} %fusion.14), channel_id=1, source_target_pairs={{0,1},{1,0},{2,3},{3,2},{4,5},{5,4},{6,7},{7,6},{8,9},{9,8},{10,11... | collective-permute-start | bytes 2752520 | tf_op jit(solution)/shard_map/ppermute | solution.py:295
  202.6 16.5 %copy-start.2 = (bf16[4,256,1792]{2,1,0:T(8,128)(2,1)S(1)}, bf16[4,256,1792]{2,1,0:T(8,128)(2,1)}, u32[]{:S(2)}) copy-start(bf16[4,256,1792]{2,1,0:T(8,128)(2,1)} %get-tuple-element.21) | copy-start | bytes 11010052
  224.8 14.0 %copy-start.8 = (bf16[4,256,1792]{2,1,0:T(8,128)(2,1)S(1)}, bf16[4,256,1792]{2,1,0:T(8,128)(2,1)}, u32[]{:S(2)}) copy-start(bf16[4,256,1792]{2,1,0:T(8,128)(2,1)} %get-tuple-element.24) | copy-start | bytes 11010052
  224.8 14.0 %copy-start.13 = (bf16[1,2,512,256]{3,2,1,0:T(8,128)(2,1)S(1)}, bf16[1,2,512,256]{3,2,1,0:T(8,128)(2,1)}, u32[]{:S(2)}) copy-start(bf16[1,2,512,256]{3,2,1,0:T(8,128)(2,1)} %get-tuple-element.35) | copy-start | bytes 1572868
  224.8 35.9 %collective-permute-start.2 = (bf16[256,1792]{1,0:T(8,128)(2,1)}, bf16[256,1792]{1,0:T(8,128)(2,1)S(1)}, u32[]{:S(2)}, u32[]{:S(2)}) collective-permute-start(bf16[256,1792]{1,0:T(8,128)(2,1)} %add_convert_fusion.1), channel_id=1, source_target_pairs={{0,2},{1,3},{2,0},{3,1},{4,6},{5,7},{6,4},{7,5},{8,10},{9,11},{10,... | collective-permute-start | bytes 2752520 | tf_op jit(solution)/shard_map/ppermute | solution.py:295
  (1 other events, 1.0 us)
